TPU v7x, 256 devices: a whole 4x4x8 slice. The times are simulated.
256 devices in a mesh: section: 16 (over y_lo, z), ctx: 16 (over y_hi, x, core).
Axes of the slice: x: 4, y: 4 (y_hi: 2, y_lo: 2; y = y_hi * 2 + y_lo), z: 8, core: 2. Of those that a mesh axis runs over, the one named last changes fastest.
Arguments:
- projected_up: bfloat16 [16, 2048, 3, 6144], P('section', 'ctx'), may hold values from -12 to 12
- projected_down: bfloat16 [16, 2048, 3, 6144], P('section', 'ctx'), may hold values from -12 to 12
- lengths_up: int32 [16, 8], P('section'), may hold values from 16 to 1024, as said below
- lengths_down: int32 [16, 8], P('section'), may hold values from 16 to 1024, as said below
- pattern_up: int32 [16, 16, 16], P('section'), may hold values from 0 to 1, as said below
- pattern_down: int32 [16, 16, 16], P('section'), may hold values from 0 to 1, as said below
Outputs:
- attended_up: bfloat16 [16, 2048, 6144], P('section', 'ctx')
- attended_down: bfloat16 [16, 2048, 6144], P('section', 'ctx')
Inputs may be any that keep to these rules, and one draw needn't show every extreme that they name: `lengths_up`: each section's 8 lengths are multiples of 16 and sum to 2048; the last one is 16, and exactly one of them is 1024. `lengths_down`: each section's 8 lengths are multiples of 16 and sum to 2048; the last one is 16, and exactly one of them is 1024. `pattern_up`: entries are 0 or 1 and the diagonal is 1. `pattern_down`: entries are 0 or 1 and the diagonal is 1.
All inputs are finite; a program needn't handle non-finite values.
Results may differ from a plain program's by a relative error of at most 0.0033.
Values may be sent and summed in bfloat16 or wider, within the bound.
No kernel may reach another device: no remote copies, remote signals or barrier semaphores. Data moves between devices by JAX's collectives and lax.ppermute only.
A program may use at most 128 MiB of HBM per device.

v0:
```python
import math

import jax
import jax.numpy as jnp
from jax import lax
from jax.sharding import PartitionSpec as P

HEAD_DIM = 128
BLOCK = 128


masked_score = -1e30


def shifted(value, axis, steps):
    count = lax.axis_size(axis)
    pairs = [(source, (source + steps) % count) for source in range(count)]
    return lax.ppermute(value, axis, pairs)


def segment_labels(lengths, token_count):
    bounds = jnp.cumsum(lengths)
    positions = jnp.arange(token_count, dtype=jnp.int32)
    return jnp.sum((positions[:, None] >= bounds[None, :]).astype(jnp.int32), axis=1)


def allowed_mask(lengths, pattern):
    token_count = pattern.shape[0] * BLOCK
    labels = segment_labels(lengths, token_count)
    widened = jnp.repeat(jnp.repeat(pattern, BLOCK, axis=0), BLOCK, axis=1)
    return (widened == 1) & (labels[:, None] == labels[None, :])


def head_attention(operands, allowed):
    queries, key_rows, value_rows = operands
    scores = lax.dot_general(
        queries, key_rows, (((1,), (1,)), ((), ())), preferred_element_type=jnp.float32
    )
    scores = scores * (1.0 / math.sqrt(HEAD_DIM))
    scores = jnp.where(allowed, scores, masked_score)
    largest = jnp.max(scores, axis=1, keepdims=True)
    exponentials = jnp.exp(scores - largest)
    totals = jnp.sum(exponentials, axis=1, keepdims=True)
    weights = exponentials.astype(jnp.bfloat16)
    combined = jnp.dot(weights, value_rows, preferred_element_type=jnp.float32)
    return (combined / totals).astype(jnp.bfloat16)


def attend_head_groups(layout, lengths, pattern):
    allowed = allowed_mask(lengths, pattern)
    per_head = layout.transpose(1, 2, 0, 3)
    result = lax.map(
        lambda operands: head_attention(operands, allowed), (per_head[0], per_head[1], per_head[2])
    )
    return result.transpose(1, 0, 2)


def per_device(projected_up, projected_down, lengths_up, lengths_down, pattern_up, pattern_down):
    local_rows = projected_up.shape[1]

    def head_layout(projected):
        return projected.reshape(1, local_rows, 3, projected.shape[3] // HEAD_DIM, HEAD_DIM)

    upper = shifted((projected_up, lengths_up, pattern_up), "section", 1)
    lower = shifted((projected_down, lengths_down, pattern_down), "section", -1)
    whole_up = lax.all_to_all(head_layout(upper[0]), "ctx", split_axis=3, concat_axis=1, tiled=True)
    whole_down = lax.all_to_all(
        head_layout(lower[0]), "ctx", split_axis=3, concat_axis=1, tiled=True
    )
    result_up = attend_head_groups(whole_up[0], upper[1][0], upper[2][0])
    result_down = attend_head_groups(whole_down[0], lower[1][0], lower[2][0])
    back_up = lax.all_to_all(result_up[None], "ctx", split_axis=1, concat_axis=2, tiled=True)
    back_down = lax.all_to_all(result_down[None], "ctx", split_axis=1, concat_axis=2, tiled=True)
    return (back_up.reshape(1, local_rows, -1), back_down.reshape(1, local_rows, -1))


def solution(mesh):
    in_specs = (
        P("section", "ctx", None, None),
        P("section", "ctx", None, None),
        P("section", None),
        P("section", None),
        P("section", None, None),
        P("section", None, None),
    )
    out_specs = (P("section", "ctx", None), P("section", "ctx", None))
    return jax.shard_map(
        per_device, mesh=mesh, in_specs=in_specs, out_specs=out_specs, check_vma=False
    )
```

profile of v0, /device:TPU:2, one launch (start us, length us, event | category | flops | bytes accessed | tf_op | source)
XLA Modules:
  0.0 388.4 jit_solution(11726506974975991621)
XLA Ops:
  0.6 6.7 %copy.54 = bf16[1,128,3,6144]{1,3,2,0:T(8,128)(2,1)} copy(bf16[1,128,3,6144]{3,1,2,0:T(8,128)(2,1)} %param.11) | data formatting | bytes 9437184 | tf_op args[1]
  7.3 6.9 %collective-permute-start.3 = (bf16[1,128,3,6144]{1,3,2,0:T(8,128)(2,1)}, bf16[1,128,3,6144]{1,3,2,0:T(8,128)(2,1)}, u32[]{:S(2)}, u32[]{:S(2)}) collective-permute-start(bf16[1,128,3,6144]{1,3,2,0:T(8,128)(2,1)} %copy.54), channel_id=1, source_target_pairs={{0,240},{16,0},{32,16},{48,32},{64,48},{80,64},{96,80},{112,96},{1... | collective-permute-start | bytes 14155784 | tf_op jit(solution)/shard_map/ppermute | solution.py:18
  14.2 6.7 %copy.46 = bf16[1,128,3,6144]{1,3,2,0:T(8,128)(2,1)} copy(bf16[1,128,3,6144]{3,1,2,0:T(8,128)(2,1)} %param.10) | data formatting | bytes 9437184 | tf_op args[0]
  20.9 94.7 %collective-permute-done.3 = bf16[1,128,3,6144]{1,3,2,0:T(8,128)(2,1)} collective-permute-done((bf16[1,128,3,6144]{1,3,2,0:T(8,128)(2,1)}, bf16[1,128,3,6144]{1,3,2,0:T(8,128)(2,1)}, u32[]{:S(2)}, u32[]{:S(2)}) %collective-permute-start.3) | collective-permute-done | bytes 4718624 | tf_op jit(solution)/shard_map/ppermute | solution.py:18
  115.6 6.3 %copy.55 = bf16[1,128,3,48,128]{1,4,2,0,3:T(8,128)(2,1)} copy(bf16[1,128,3,48,128]{1,4,3,2,0:T(8,128)(2,1)} %bitcast.17) | data formatting | bytes 9437184 | tf_op jit(solution)/shard_map/reshape | solution.py:62
  121.9 7.2 %all-to-all-start.2 = ((bf16[1,128,3,48,128]{1,4,2,0,3:T(8,128)(2,1)}), bf16[1,128,3,48,128]{1,4,2,0,3:T(8,128)(2,1)}, u32[]{:S(2)}, u32[]{:S(2)}) async-start(bf16[1,128,3,48,128]{1,4,2,0,3:T(8,128)(2,1)} %copy.55), calls=%async_computation.2 | async-start | bytes 9437184 | tf_op jit(solution)/shard_map/all_to_all | solution.py:67
  129.1 6.3 %copy.47 = bf16[1,128,3,48,128]{1,4,2,0,3:T(8,128)(2,1)} copy(bf16[1,128,3,48,128]{1,4,3,2,0:T(8,128)(2,1)} %bitcast) | data formatting | bytes 9437184 | tf_op jit(solution)/shard_map/reshape | solution.py:62
  135.4 57.8 %all-to-all-done.2 = bf16[1,128,3,48,128]{1,4,2,0,3:T(8,128)(2,1)} async-done(((bf16[1,128,3,48,128]{1,4,2,0,3:T(8,128)(2,1)}), bf16[1,128,3,48,128]{1,4,2,0,3:T(8,128)(2,1)}, u32[]{:S(2)}, u32[]{:S(2)}) %all-to-all-start.2) | async-done | bytes 4718624 | tf_op jit(solution)/shard_map/all_to_all | solution.py:67
  193.2 5.4 %all-to-all-start = ((bf16[1,128,3,48,128]{1,4,2,0,3:T(8,128)(2,1)}), bf16[1,128,3,48,128]{1,4,2,0,3:T(8,128)(2,1)}, u32[]{:S(2)}, u32[]{:S(2)}) async-start(bf16[1,128,3,48,128]{1,4,2,0,3:T(8,128)(2,1)} %copy.47), calls=%async_computation | async-start | bytes 9437184 | tf_op jit(solution)/shard_map/all_to_all | solution.py:66
  206.4 5.5 %collective-permute-done.2 = s32[1,8]{1,0:T(1,128)S(1)} collective-permute-done((s32[1,8]{1,0:T(1,128)S(1)}, s32[1,8]{1,0:T(1,128)S(1)}, u32[]{:S(2)}, u32[]{:S(2)}) %collective-permute-start.2) | collective-permute-done | bytes 64 | tf_op jit(solution)/shard_map/ppermute | solution.py:18
  212.7 6.7 %copy.56 = bf16[1,128,3,48,128]{4,1,3,2,0:T(8,128)(2,1)} copy(bf16[1,128,3,48,128]{1,4,2,0,3:T(8,128)(2,1)} %all-to-all-done.2) | data formatting | bytes 9437184 | tf_op jit(solution)/shard_map/all_to_all | solution.py:67
  225.6 46.7 %while.23 = (s32[]{:T(128)}, bf16[3,2048,128]{2,1,0:T(8,128)(2,1)}, bf16[3,2048,128]{2,1,0:T(8,128)(2,1)S(1)}, bf16[3,2048,128]{2,1,0:T(8,128)(2,1)S(1)}, bf16[3...) while((s32[]{:T(128)}, bf16[3,2048,128]{2,1,0:T(8,128)(2,1)}, ...), condition=%wide.region_11.12_spmd.clone, body=%wide.region_8.11_spmd.clone.sunk | while | flops 2198335488 | bytes 52553812 | solution.py:52
  225.6 4.2 %fusion.53 = (f32[2048]{0:T(1024)S(1)}, f32[2048,2048]{0,1:T(8,128)S(1)}) fusion(s32[2048]{0:T(1024)S(1)} %get-tuple-element.302, pred[2048,16]{0,1:T(8,128)(4,1)S(1)} %get-tuple-element.301, bf16[3,2048,128]{2,1,0:T(8,128)(2,1)S(1)} %get-tuple-element.299, s32[]{:T(128)} %get-tuple-element.288, bf16[3,2048,128]{2,1,0:T(8,128)(2,1)S(1)} %get-tuple-element.298), kind=kOutput, calls=%fused_computation.26.clone.1 | convolution fusion | flops 1094711296 | bytes 17884160 | tf_op jit(solution)/shard_map/while/body/eval_jaxpr/dot_general | solution.py:36
  229.8 6.9 %fusion.54 = (f32[2048]{0:T(1024)S(1)}, bf16[2048,2048]{0,1:T(8,128)(2,1)S(1)}) fusion(f32[2048,2048]{0,1:T(8,128)S(1)} %get-tuple-element.252, s32[2048]{0:T(1024)S(1)} %get-tuple-element.302, f32[2048]{0:T(1024)S(1)} %get-tuple-element.253, pred[2048,16]{0,1:T(8,128)(4,1)S(1)} %get-tuple-element.301), kind=kLoop, calls=%fused_computation.24.clone.1 | loop fusion | flops 29358080 | bytes 25223168 | tf_op jit(solution)/shard_map/while/body/eval_jaxpr/reduce_sum | solution.py:43
  236.8 4.4 %fusion.55 = bf16[3,2048,128]{2,1,0:T(8,128)(2,1)} fusion(bf16[3,2048,128]{2,1,0:T(8,128)(2,1)} %get-tuple-element.289, s32[]{:T(128)} %get-tuple-element.288, bf16[2048,2048]{0,1:T(8,128)(2,1)S(1)} %get-tuple-element.254, f32[2048]{0:T(1024)S(1)} %get-tuple-element.255, bf16[3,2048,128]{2,1,0:T(8,128)(2,1)} %get-tuple-element.300), kind=kOutput, calls=%fused_computation.30.clone.1 | convolution fusion | flops 1074266112 | bytes 9446400 | tf_op jit(solution)/shard_map/while/body/eval_jaxpr/dot_general | solution.py:45
  241.1 4.2 %fusion.53 = (f32[2048]{0:T(1024)S(1)}, f32[2048,2048]{0,1:T(8,128)S(1)}) fusion(s32[2048]{0:T(1024)S(1)} %get-tuple-element.302, pred[2048,16]{0,1:T(8,128)(4,1)S(1)} %get-tuple-element.301, bf16[3,2048,128]{2,1,0:T(8,128)(2,1)S(1)} %get-tuple-element.299, s32[]{:T(128)} %get-tuple-element.288, bf16[3,2048,128]{2,1,0:T(8,128)(2,1)S(1)} %get-tuple-element.298), kind=kOutput, calls=%fused_computation.26.clone.1 | convolution fusion | flops 1094711296 | bytes 17884160 | tf_op jit(solution)/shard_map/while/body/eval_jaxpr/dot_general | solution.py:36
  245.4 6.9 %fusion.54 = (f32[2048]{0:T(1024)S(1)}, bf16[2048,2048]{0,1:T(8,128)(2,1)S(1)}) fusion(f32[2048,2048]{0,1:T(8,128)S(1)} %get-tuple-element.252, s32[2048]{0:T(1024)S(1)} %get-tuple-element.302, f32[2048]{0:T(1024)S(1)} %get-tuple-element.253, pred[2048,16]{0,1:T(8,128)(4,1)S(1)} %get-tuple-element.301), kind=kLoop, calls=%fused_computation.24.clone.1 | loop fusion | flops 29358080 | bytes 25223168 | tf_op jit(solution)/shard_map/while/body/eval_jaxpr/reduce_sum | solution.py:43
  252.3 4.4 %fusion.55 = bf16[3,2048,128]{2,1,0:T(8,128)(2,1)} fusion(bf16[3,2048,128]{2,1,0:T(8,128)(2,1)} %get-tuple-element.289, s32[]{:T(128)} %get-tuple-element.288, bf16[2048,2048]{0,1:T(8,128)(2,1)S(1)} %get-tuple-element.254, f32[2048]{0:T(1024)S(1)} %get-tuple-element.255, bf16[3,2048,128]{2,1,0:T(8,128)(2,1)} %get-tuple-element.300), kind=kOutput, calls=%fused_computation.30.clone.1 | convolution fusion | flops 1074266112 | bytes 9446400 | tf_op jit(solution)/shard_map/while/body/eval_jaxpr/dot_general | solution.py:45
  256.7 4.2 %fusion.53 = (f32[2048]{0:T(1024)S(1)}, f32[2048,2048]{0,1:T(8,128)S(1)}) fusion(s32[2048]{0:T(1024)S(1)} %get-tuple-element.302, pred[2048,16]{0,1:T(8,128)(4,1)S(1)} %get-tuple-element.301, bf16[3,2048,128]{2,1,0:T(8,128)(2,1)S(1)} %get-tuple-element.299, s32[]{:T(128)} %get-tuple-element.288, bf16[3,2048,128]{2,1,0:T(8,128)(2,1)S(1)} %get-tuple-element.298), kind=kOutput, calls=%fused_computation.26.clone.1 | convolution fusion | flops 1094711296 | bytes 17884160 | tf_op jit(solution)/shard_map/while/body/eval_jaxpr/dot_general | solution.py:36
  261.0 6.9 %fusion.54 = (f32[2048]{0:T(1024)S(1)}, bf16[2048,2048]{0,1:T(8,128)(2,1)S(1)}) fusion(f32[2048,2048]{0,1:T(8,128)S(1)} %get-tuple-element.252, s32[2048]{0:T(1024)S(1)} %get-tuple-element.302, f32[2048]{0:T(1024)S(1)} %get-tuple-element.253, pred[2048,16]{0,1:T(8,128)(4,1)S(1)} %get-tuple-element.301), kind=kLoop, calls=%fused_computation.24.clone.1 | loop fusion | flops 29358080 | bytes 25223168 | tf_op jit(solution)/shard_map/while/body/eval_jaxpr/reduce_sum | solution.py:43
  267.9 4.4 %fusion.55 = bf16[3,2048,128]{2,1,0:T(8,128)(2,1)} fusion(bf16[3,2048,128]{2,1,0:T(8,128)(2,1)} %get-tuple-element.289, s32[]{:T(128)} %get-tuple-element.288, bf16[2048,2048]{0,1:T(8,128)(2,1)S(1)} %get-tuple-element.254, f32[2048]{0:T(1024)S(1)} %get-tuple-element.255, bf16[3,2048,128]{2,1,0:T(8,128)(2,1)} %get-tuple-element.300), kind=kOutput, calls=%fused_computation.30.clone.1 | convolution fusion | flops 1074266112 | bytes 9446400 | tf_op jit(solution)/shard_map/while/body/eval_jaxpr/dot_general | solution.py:45
  276.4 7.6 %all-to-all-start.3 = ((bf16[1,2048,3,128]{3,2,0,1:T(4,128)(2,1)}), bf16[1,2048,3,128]{3,2,0,1:T(4,128)(2,1)}, u32[]{:S(2)}, u32[]{:S(2)}) async-start(bf16[1,2048,3,128]{3,2,0,1:T(4,128)(2,1)} %bitcast.116), calls=%async_computation.3 | async-start | bytes 4194304 | tf_op jit(solution)/shard_map/all_to_all | solution.py:73
  284.0 6.7 %copy.48 = bf16[1,128,3,48,128]{4,1,3,2,0:T(8,128)(2,1)} copy(bf16[1,128,3,48,128]{1,4,2,0,3:T(8,128)(2,1)} %all-to-all-done) | data formatting | bytes 9437184 | tf_op jit(solution)/shard_map/all_to_all | solution.py:66
  296.9 46.6 %while.22 = (s32[]{:T(128)}, bf16[3,2048,128]{2,1,0:T(8,128)(2,1)}, bf16[3,2048,128]{2,1,0:T(8,128)(2,1)S(1)}, bf16[3,2048,128]{2,1,0:T(8,128)(2,1)S(1)}, bf16[3...) while((s32[]{:T(128)}, bf16[3,2048,128]{2,1,0:T(8,128)(2,1)}, ...), condition=%wide.region_5.6_spmd.clone, body=%wide.region_2.5_spmd.clone.sunk | while | flops 2198335488 | bytes 52553812 | solution.py:52
  301.1 6.9 %fusion.49 = (f32[2048]{0:T(1024)S(1)}, bf16[2048,2048]{0,1:T(8,128)(2,1)S(1)}) fusion(f32[2048,2048]{0,1:T(8,128)S(1)} %get-tuple-element.241, s32[2048]{0:T(1024)S(1)} %get-tuple-element.278, f32[2048]{0:T(1024)S(1)} %get-tuple-element.242, pred[2048,16]{0,1:T(8,128)(4,1)S(1)} %get-tuple-element.277), kind=kLoop, calls=%fused_computation.5.clone.1 | loop fusion | flops 29358080 | bytes 25223168 | tf_op jit(solution)/shard_map/while/body/eval_jaxpr/reduce_sum | solution.py:43
  308.0 4.4 %fusion.50 = bf16[3,2048,128]{2,1,0:T(8,128)(2,1)} fusion(bf16[3,2048,128]{2,1,0:T(8,128)(2,1)} %get-tuple-element.265, s32[]{:T(128)} %get-tuple-element.264, bf16[2048,2048]{0,1:T(8,128)(2,1)S(1)} %get-tuple-element.243, f32[2048]{0:T(1024)S(1)} %get-tuple-element.244, bf16[3,2048,128]{2,1,0:T(8,128)(2,1)} %get-tuple-element.276), kind=kOutput, calls=%fused_computation.11.clone.1 | convolution fusion | flops 1074266112 | bytes 9446400 | tf_op jit(solution)/shard_map/while/body/eval_jaxpr/dot_general | solution.py:45
  316.6 6.9 %fusion.49 = (f32[2048]{0:T(1024)S(1)}, bf16[2048,2048]{0,1:T(8,128)(2,1)S(1)}) fusion(f32[2048,2048]{0,1:T(8,128)S(1)} %get-tuple-element.241, s32[2048]{0:T(1024)S(1)} %get-tuple-element.278, f32[2048]{0:T(1024)S(1)} %get-tuple-element.242, pred[2048,16]{0,1:T(8,128)(4,1)S(1)} %get-tuple-element.277), kind=kLoop, calls=%fused_computation.5.clone.1 | loop fusion | flops 29358080 | bytes 25223168 | tf_op jit(solution)/shard_map/while/body/eval_jaxpr/reduce_sum | solution.py:43
  323.5 4.4 %fusion.50 = bf16[3,2048,128]{2,1,0:T(8,128)(2,1)} fusion(bf16[3,2048,128]{2,1,0:T(8,128)(2,1)} %get-tuple-element.265, s32[]{:T(128)} %get-tuple-element.264, bf16[2048,2048]{0,1:T(8,128)(2,1)S(1)} %get-tuple-element.243, f32[2048]{0:T(1024)S(1)} %get-tuple-element.244, bf16[3,2048,128]{2,1,0:T(8,128)(2,1)} %get-tuple-element.276), kind=kOutput, calls=%fused_computation.11.clone.1 | convolution fusion | flops 1074266112 | bytes 9446400 | tf_op jit(solution)/shard_map/while/body/eval_jaxpr/dot_general | solution.py:45
  332.2 6.9 %fusion.49 = (f32[2048]{0:T(1024)S(1)}, bf16[2048,2048]{0,1:T(8,128)(2,1)S(1)}) fusion(f32[2048,2048]{0,1:T(8,128)S(1)} %get-tuple-element.241, s32[2048]{0:T(1024)S(1)} %get-tuple-element.278, f32[2048]{0:T(1024)S(1)} %get-tuple-element.242, pred[2048,16]{0,1:T(8,128)(4,1)S(1)} %get-tuple-element.277), kind=kLoop, calls=%fused_computation.5.clone.1 | loop fusion | flops 29358080 | bytes 25223168 | tf_op jit(solution)/shard_map/while/body/eval_jaxpr/reduce_sum | solution.py:43
  339.1 4.4 %fusion.50 = bf16[3,2048,128]{2,1,0:T(8,128)(2,1)} fusion(bf16[3,2048,128]{2,1,0:T(8,128)(2,1)} %get-tuple-element.265, s32[]{:T(128)} %get-tuple-element.264, bf16[2048,2048]{0,1:T(8,128)(2,1)S(1)} %get-tuple-element.243, f32[2048]{0:T(1024)S(1)} %get-tuple-element.244, bf16[3,2048,128]{2,1,0:T(8,128)(2,1)} %get-tuple-element.276), kind=kOutput, calls=%fused_computation.11.clone.1 | convolution fusion | flops 1074266112 | bytes 9446400 | tf_op jit(solution)/shard_map/while/body/eval_jaxpr/dot_general | solution.py:45
  347.7 7.2 %all-to-all-start.1 = ((bf16[1,2048,3,128]{3,2,0,1:T(4,128)(2,1)}), bf16[1,2048,3,128]{3,2,0,1:T(4,128)(2,1)S(1)}, u32[]{:S(2)}, u32[]{:S(2)}) async-start(bf16[1,2048,3,128]{3,2,0,1:T(4,128)(2,1)} %bitcast.117), calls=%async_computation.1 | async-start | bytes 4194304 | tf_op jit(solution)/shard_map/all_to_all | solution.py:72
  363.0 20.5 %all-to-all-done.1 = bf16[1,2048,3,128]{3,2,0,1:T(4,128)(2,1)S(1)} async-done(((bf16[1,2048,3,128]{3,2,0,1:T(4,128)(2,1)}), bf16[1,2048,3,128]{3,2,0,1:T(4,128)(2,1)S(1)}, u32[]{:S(2)}, u32[]{:S(2)}) %all-to-all-start.1) | async-done | bytes 1572896 | tf_op jit(solution)/shard_map/all_to_all | solution.py:72
  (48 shorter events, 54.8 us)
Async XLA Ops:
  7.3 108.3 %collective-permute-start.3 = (bf16[1,128,3,6144]{1,3,2,0:T(8,128)(2,1)}, bf16[1,128,3,6144]{1,3,2,0:T(8,128)(2,1)}, u32[]{:S(2)}, u32[]{:S(2)}) collective-permute-start(bf16[1,128,3,6144]{1,3,2,0:T(8,128)(2,1)} %copy.54), channel_id=1, source_target_pairs={{0,240},{16,0},{32,16},{48,32},{64,48},{80,64},{96,80},{112,96},{1... | collective-permute-start | bytes 14155784 | tf_op jit(solution)/shard_map/ppermute | solution.py:18
  20.9 108.2 %collective-permute-start = (bf16[1,128,3,6144]{1,3,2,0:T(8,128)(2,1)}, bf16[1,128,3,6144]{1,3,2,0:T(8,128)(2,1)}, u32[]{:S(2)}, u32[]{:S(2)}) collective-permute-start(bf16[1,128,3,6144]{1,3,2,0:T(8,128)(2,1)} %copy.46), channel_id=1, source_target_pairs={{0,16},{16,32},{32,48},{48,64},{64,80},{80,96},{96,112},{112,128},... | collective-permute-start | bytes 14155784 | tf_op jit(solution)/shard_map/ppermute | solution.py:18
  121.9 71.3 %all-to-all-start.2 = ((bf16[1,128,3,48,128]{1,4,2,0,3:T(8,128)(2,1)}), bf16[1,128,3,48,128]{1,4,2,0,3:T(8,128)(2,1)}, u32[]{:S(2)}, u32[]{:S(2)}) async-start(bf16[1,128,3,48,128]{1,4,2,0,3:T(8,128)(2,1)} %copy.55), calls=%async_computation.2 | async-start | bytes 9437184 | tf_op jit(solution)/shard_map/all_to_all | solution.py:67
  135.4 63.2 %copy-start = (s32[1,16,16]{2,1,0:T(8,128)S(1)}, s32[1,16,16]{2,1,0:T(8,128)}, u32[]{:S(2)}) copy-start(s32[1,16,16]{2,1,0:T(8,128)} %param.15) | copy-start | bytes 3076
  135.4 67.2 %copy-start.2 = (s32[1,8]{1,0:T(1,128)S(1)}, s32[1,8]{1,0:T(1,128)}, u32[]{:S(2)}) copy-start(s32[1,8]{1,0:T(1,128)} %param.13) | copy-start | bytes 100
  135.4 67.3 %copy-start.1 = (s32[1,16,16]{2,1,0:T(8,128)S(1)}, s32[1,16,16]{2,1,0:T(8,128)}, u32[]{:S(2)}) copy-start(s32[1,16,16]{2,1,0:T(8,128)} %param.14) | copy-start | bytes 3076
  135.4 69.3 %copy-start.3 = (s32[1,8]{1,0:T(1,128)S(1)}, s32[1,8]{1,0:T(1,128)}, u32[]{:S(2)}) copy-start(s32[1,8]{1,0:T(1,128)} %param.12) | copy-start | bytes 100
  193.2 83.3 %all-to-all-start = ((bf16[1,128,3,48,128]{1,4,2,0,3:T(8,128)(2,1)}), bf16[1,128,3,48,128]{1,4,2,0,3:T(8,128)(2,1)}, u32[]{:S(2)}, u32[]{:S(2)}) async-start(bf16[1,128,3,48,128]{1,4,2,0,3:T(8,128)(2,1)} %copy.47), calls=%async_computation | async-start | bytes 9437184 | tf_op jit(solution)/shard_map/all_to_all | solution.py:66
  198.6 13.7 %collective-permute-start.4 = (s32[1,16,16]{2,1,0:T(8,128)S(1)}, s32[1,16,16]{2,1,0:T(8,128)S(1)}, u32[]{:S(2)}, u32[]{:S(2)}) collective-permute-start(s32[1,16,16]{2,1,0:T(8,128)S(1)} %copy-done), channel_id=1, source_target_pairs={{0,240},{16,0},{32,16},{48,32},{64,48},{80,64},{96,80},{112,96},{1... | collective-permute-start | bytes 3080 | tf_op jit(solution)/shard_map/ppermute | solution.py:18
  202.6 3.5 collective-permute-start.5
  202.7 9.8 %collective-permute-start.1 = (s32[1,16,16]{2,1,0:T(8,128)S(1)}, s32[1,16,16]{2,1,0:T(8,128)S(1)}, u32[]{:S(2)}, u32[]{:S(2)}) collective-permute-start(s32[1,16,16]{2,1,0:T(8,128)S(1)} %copy-done.1), channel_id=1, source_target_pairs={{0,16},{16,32},{32,48},{48,64},{64,80},{80,96},{96,112},{112,128},... | collective-permute-start | bytes 3080 | tf_op jit(solution)/shard_map/ppermute | solution.py:18
  204.7 7.2 %collective-permute-start.2 = (s32[1,8]{1,0:T(1,128)S(1)}, s32[1,8]{1,0:T(1,128)S(1)}, u32[]{:S(2)}, u32[]{:S(2)}) collective-permute-start(s32[1,8]{1,0:T(1,128)S(1)} %copy-done.3), channel_id=1, source_target_pairs={{0,16},{16,32},{32,48},{48,64},{64,80},{80,96},{96,112},{112,128},... | collective-permute-start | bytes 104 | tf_op jit(solution)/shard_map/ppermute | solution.py:18
  276.4 71.3 %all-to-all-start.3 = ((bf16[1,2048,3,128]{3,2,0,1:T(4,128)(2,1)}), bf16[1,2048,3,128]{3,2,0,1:T(4,128)(2,1)}, u32[]{:S(2)}, u32[]{:S(2)}) async-start(bf16[1,2048,3,128]{3,2,0,1:T(4,128)(2,1)} %bitcast.116), calls=%async_computation.3 | async-start | bytes 4194304 | tf_op jit(solution)/shard_map/all_to_all | solution.py:73
  347.7 35.8 %all-to-all-start.1 = ((bf16[1,2048,3,128]{3,2,0,1:T(4,128)(2,1)}), bf16[1,2048,3,128]{3,2,0,1:T(4,128)(2,1)S(1)}, u32[]{:S(2)}, u32[]{:S(2)}) async-start(bf16[1,2048,3,128]{3,2,0,1:T(4,128)(2,1)} %bitcast.117), calls=%async_computation.1 | async-start | bytes 4194304 | tf_op jit(solution)/shard_map/all_to_all | solution.py:72
where the time goes:
time: 391 us; the launch traced here: 388 us
  waiting for transfers between devices  180 us (46%)
  local copies, waits for them, and re-layouts  73.5 us (19%)
  matrix products  51.8 us (13%)
  other arithmetic  42 us (11%)
  starting transfers between devices  40.6 us (10%)
    ppermute x6, waiting for transfers between devices, shifted(): return lax.ppermute(value, axis, pairs)  101 us
    all_to_all x1, waiting for transfers between devices, per_device(): lax.all_to_all(head_layout(lower[0]), 'ctx', split_axis=3, concat_axis=1,...  57.8 us
    reduce_sum x6, other arithmetic, head_attention(): totals = jnp.sum(exponentials, axis=1, keepdims=True)  41.4 us
    dot_general x6, matrix products, head_attention(): combined = jnp.dot(weights, value_rows, preferred_element_type=jnp.float32)  26.4 us
    dot_general x6, matrix products, head_attention(): lax.dot_general(queries, key_rows, (((1,), (1,)), ((), ())), preferred_el...  25.4 us
    all_to_all x1, waiting for transfers between devices, per_device(): lax.all_to_all(result_up[None], 'ctx', split_axis=1, concat_axis=2, tiled...  20.5 us
    unnamed x14, local copies, waits for them, and re-layouts  17.6 us
    ppermute x6, starting transfers between devices, shifted(): return lax.ppermute(value, axis, pairs)  13.2 us
  transfers between devices with their start and end apart: 10, of which 5 were waited for; matrix products, arithmetic and copies ran while one was open for 40% of the time, Pallas kernels for 0%

commit v1 on v0

v1 whole, which is shorter than its diff:
```python
import functools
import math

import jax
import jax.numpy as jnp
from jax import lax
from jax.experimental import pallas as pl
from jax.experimental.pallas import tpu as pltpu
from jax.sharding import PartitionSpec as P

HEAD_DIM = 128
BLOCK = 128
TALL = 2
WIDE = 4
GROUP = 3
CHIPS = 4
CUT_VMEM = 60 * 1024 * 1024

masked_score = -1e30
exponent_scale = math.log2(math.e) / math.sqrt(HEAD_DIM)

IN_HBM = pl.BlockSpec(memory_space=pl.ANY)
IN_SMEM = pl.BlockSpec(memory_space=pltpu.SMEM)


def carry(sources, targets, held, arrived, left):
    arrivals, departures = [], []
    for slot, (source, target) in enumerate(zip(sources, targets)):
        arrivals.append(pltpu.make_async_copy(source, held.at[slot], arrived.at[slot]))
        departures.append(pltpu.make_async_copy(held.at[slot], target, left.at[slot]))
    for arrival in arrivals:
        arrival.start()
    for arrival, departure in zip(arrivals, departures):
        arrival.wait()
        departure.start()
    for departure in departures:
        departure.wait()


def carry_scratch(count, shape):
    return [
        pltpu.VMEM((count, *shape), jnp.bfloat16),
        pltpu.SemaphoreType.DMA((count,)),
        pltpu.SemaphoreType.DMA((count,)),
    ]


def columns_of(side, place, offset, width):
    chip = side * CHIPS + (place ^ offset)
    return pl.ds(pl.multiple_of(chip * width, width), width)


def copied(plan, inputs, shapes, position, name, piece=None):
    piece = piece or shapes[0][-3:]
    count = len(plan(None, [None] * len(inputs), [None] * len(shapes), True))

    def kernel(position, *refs):
        ins, outs = refs[: len(inputs)], refs[len(inputs) : len(inputs) + len(shapes)]
        pairs = plan(position, ins, outs, False)
        carry([pair[0] for pair in pairs], [pair[1] for pair in pairs], *refs[-3:])

    return pl.pallas_call(
        kernel,
        out_shape=[jax.ShapeDtypeStruct(shape, jnp.bfloat16) for shape in shapes],
        in_specs=[IN_SMEM] + [IN_HBM] * len(inputs),
        out_specs=[IN_HBM] * len(shapes),
        scratch_shapes=carry_scratch(count, piece),
        compiler_params=pltpu.CompilerParams(vmem_limit_bytes=CUT_VMEM),
        name=name,
    )(position, *inputs)


def cut_from(rows, position, side, offset, width):
    return rows.at[:, :, columns_of(position[0] ^ side, position[1], offset, width)]


def cut_side(rows, position, piece, side):
    def plan(position, ins, outs, dry):
        if dry:
            return range(CHIPS)
        return [
            (cut_from(ins[0], position, side, offset, piece[-1]), outs[0].at[offset])
            for offset in range(CHIPS)
        ]

    return copied(plan, [rows], [(CHIPS, *piece)], position, "cut_side")[0]


def cut_both(up, down, position, piece, offsets):
    def plan(position, ins, outs, dry):
        if dry:
            return range(2 * len(offsets))
        pairs = []
        for out, offset in zip(outs, offsets):
            for part in range(2):
                source = cut_from(ins[part], position, part, offset, piece[-1])
                pairs.append((source, out.at[part]))
        return pairs

    return copied(plan, [up, down], [(2, *piece)] * len(offsets), position, "cut_both")


def cut_each(rows, position, piece, side):
    def plan(position, ins, outs, dry):
        if dry:
            return range(CHIPS)
        return [
            (cut_from(ins[0], position, side, offset, piece[-1]), outs[offset])
            for offset in range(CHIPS)
        ]

    return copied(plan, [rows], [piece] * CHIPS, position, "cut_each")


def regroup(spread, position):
    piece = spread[0].shape[1:]

    def plan(position, ins, outs, dry):
        if dry:
            return range(2 * CHIPS)
        return [
            (ins[index].at[side], outs[side].at[index])
            for side in (1, 0)
            for index in range(CHIPS)
        ]

    return copied(plan, spread, [(CHIPS, *piece)] * 2, position, "regroup")


def separate(pieces, position):
    shape = pieces.shape[1:]

    def plan(position, ins, outs, dry):
        if dry:
            return range(CHIPS - 1)
        return [(ins[0].at[index + 1], outs[index]) for index in range(CHIPS - 1)]

    return copied(plan, [pieces], [shape] * (CHIPS - 1), position, "separate")


def gather(sources, position):
    arrays = [array for array, _ in sources]
    piece = (2, *arrays[0].shape[-2:])

    def plan(position, ins, outs, dry):
        if dry:
            return range(CHIPS)
        return [
            (part(ins[index], where).at[pl.ds(1, 2)], outs[0].at[index])
            for index, (_, where) in enumerate(sources)
        ]

    return copied(plan, arrays, [(CHIPS, *piece)], position, "gather")[0]


def part(ref, where):
    return ref if where is None else ref.at[where]


def join(pieces, position):
    tokens, width = pieces[0].shape
    count = len(pieces)

    def plan(position, ins, outs, dry):
        if dry:
            return range(count)
        if len(ins) == 1:
            return [
                (ins[0].at[chip], outs[0].at[:, pl.ds(chip * width, width)])
                for chip in range(count)
            ]
        pairs = []
        for index, ref in enumerate(ins):
            side, offset = index // CHIPS, index % CHIPS
            columns = columns_of(position[0] ^ side, position[1], offset, width)
            pairs.append((ref, outs[0].at[:, columns]))
        return pairs

    inputs = pieces if isinstance(pieces, list) else [pieces]
    shape = (tokens, count * width)
    return copied(plan, inputs, [shape], position, "join", (tokens, width))[0]


def attend_kernel(places, apart, lengths, pattern, position, *refs):
    pieces = refs[: 2 * CHIPS]
    near_other, far_other = refs[2 * CHIPS : 2 * CHIPS + 2]
    scratch = refs[-9:] if apart else refs[-8:]
    asked, held, scores, largest, totals, combined, listed, arrived = scratch[-8:]
    outs = refs[2 * CHIPS + 2 : -len(scratch)]
    out_ref = scratch[0] if apart else outs[0]
    blocks = held.shape[0]
    group_heads = largest.shape[0]
    tile = TALL * BLOCK
    core = position[2]

    def block_of(piece, core):
        return (position[0] ^ (piece // CHIPS)) * (2 * CHIPS) + (
            (position[1] ^ (piece % CHIPS)) * 2 + core
        )

    copies = []
    for piece in range(2 * CHIPS):
        chip = block_of(piece, core) // 2
        copies.append((part(pieces[piece], places[piece]).at[0], asked.at[chip]))
        mine = part(pieces[piece], places[piece]).at[pl.ds(1, 2)]
        copies.append((mine, held.at[block_of(piece, core)]))
        other = (near_other if piece < CHIPS else far_other).at[piece % CHIPS]
        if other.shape[0] == 3:
            other = other.at[pl.ds(1, 2)]
        copies.append((other, held.at[block_of(piece, 1 - core)]))
    copies = [
        pltpu.make_async_copy(source, target, arrived.at[index])
        for index, (source, target) in enumerate(copies)
    ]
    for copy in copies:
        copy.start()

    bounds = []
    bound = jnp.int32(0)
    for clip in range(lengths.shape[0]):
        bound = bound + lengths[clip]
        bounds.append(bound)

    def labels(tokens):
        found = jnp.zeros(tokens.shape, jnp.int32)
        for bound in bounds:
            found = found + (tokens >= bound).astype(jnp.int32)
        return found

    for copy in copies:
        copy.wait()

    def rows(step, _):
        own = [(step * TALL + row) * 2 + core for row in range(TALL)]
        first, last = own[0] * BLOCK, own[-1] * BLOCK + BLOCK - 1
        low, high = jnp.int32(0), bounds[-1]
        for bound in bounds:
            low = jnp.where(bound <= first, bound, low)
        for bound in reversed(bounds):
            high = jnp.where(bound > last, bound, high)

        def look(column, count):
            listed[count] = column
            taken = pattern[own[0], column]
            for block in own[1:]:
                taken = taken | pattern[block, column]
            return count + taken

        count = lax.fori_loop(low // BLOCK, (high + BLOCK - 1) // BLOCK, look, jnp.int32(0))
        for extra in range(WIDE - 1):
            listed[count + extra] = -1
        steps = (count + WIDE - 1) // WIDE

        tokens = lax.broadcasted_iota(jnp.int32, (BLOCK, BLOCK), 0)
        row_labels = [labels(block * BLOCK + tokens) for block in own]
        lanes = lax.broadcasted_iota(jnp.int32, (1, BLOCK), 1)

        def heads(group, _):
            largest[...] = jnp.full(largest.shape, masked_score, jnp.float32)
            totals[...] = jnp.zeros(totals.shape, jnp.float32)
            combined[...] = jnp.zeros(combined.shape, jnp.float32)

            def columns_of_head(head):
                start = (group * group_heads + head) * HEAD_DIM
                return pl.ds(pl.multiple_of(start, HEAD_DIM), HEAD_DIM)

            def score(chunk, _):
                columns, allowed = [], []
                for part in range(WIDE):
                    entry = listed[chunk * WIDE + part]
                    column = jnp.maximum(entry, 0)
                    columns.append(column)
                    found = jnp.where(entry < 0, -1, labels(column * BLOCK + lanes))
                    allowed.append(
                        jnp.concatenate(
                            [
                                row_labels[row] == jnp.where(pattern[block, column] == 1, found, -1)
                                for row, block in enumerate(own)
                            ],
                            axis=0,
                        )
                    )
                for head in range(group_heads):
                    at = columns_of_head(head)
                    queries = asked[pl.ds(step * TALL, TALL), :, at].reshape(tile, HEAD_DIM)
                    keys = jnp.concatenate([held[column, 0, :, at] for column in columns], axis=0)
                    found = lax.dot_general(
                        queries, keys, (((1,), (1,)), ((), ())), preferred_element_type=jnp.float32
                    )
                    top = largest[head]
                    for part in range(WIDE):
                        span = slice(part * BLOCK, (part + 1) * BLOCK)
                        masked = jnp.where(allowed[part], found[:, span], masked_score)
                        scores[head, chunk, :, span] = masked
                        top = jnp.maximum(top, masked)
                    largest[head] = top
                return 0

            lax.fori_loop(0, steps, score, 0)
            for head in range(group_heads):
                largest[head] = jnp.broadcast_to(
                    jnp.max(largest[head], axis=1, keepdims=True), (tile, BLOCK)
                )

            def combine(chunk, _):
                columns = [jnp.maximum(listed[chunk * WIDE + part], 0) for part in range(WIDE)]
                for head in range(group_heads):
                    at = columns_of_head(head)
                    top, total, weights = largest[head], totals[head], []
                    for part in range(WIDE):
                        span = slice(part * BLOCK, (part + 1) * BLOCK)
                        powers = jnp.exp2((scores[head, chunk, :, span] - top) * exponent_scale)
                        total = total + powers
                        weights.append(powers.astype(jnp.bfloat16))
                    totals[head] = total
                    values = jnp.concatenate([held[column, 1, :, at] for column in columns], axis=0)
                    combined[head] += jnp.dot(
                        jnp.concatenate(weights, axis=1), values, preferred_element_type=jnp.float32
                    )
                return 0

            lax.fori_loop(0, steps, combine, 0)
            for head in range(group_heads):
                total = jnp.sum(totals[head], axis=1, keepdims=True)
                result = (combined[head] / total).astype(jnp.bfloat16)
                out_ref[pl.ds(step * TALL, TALL), :, columns_of_head(head)] = result.reshape(
                    TALL, BLOCK, HEAD_DIM
                )
            return 0

        lax.fori_loop(0, out_ref.shape[2] // (group_heads * HEAD_DIM), heads, 0)
        return 0

    lax.fori_loop(0, 2 * CHIPS // TALL, rows, 0)
    if apart:
        copies = [
            pltpu.make_async_copy(out_ref.at[block_of(slot, core) // 2], out, arrived.at[slot])
            for slot, out in enumerate(outs)
        ]
        for copy in copies:
            copy.start()
        for copy in copies:
            copy.wait()


def attend(pieces, near_other, far_other, position, lengths, pattern, apart):
    places = [where for _, where in pieces]
    pieces = [array for array, _ in pieces]
    kinds, _, width = pieces[0].shape[-3:]
    blocks, tile = 4 * CHIPS, TALL * BLOCK
    heads, count = width // HEAD_DIM, 2 * CHIPS
    per_head = pltpu.VMEM((GROUP, tile, BLOCK), jnp.float32)

    def kernel(*refs):
        attend_kernel(places, apart, *refs)

    return pl.pallas_call(
        kernel,
        out_shape=[jax.ShapeDtypeStruct((BLOCK, width), jnp.bfloat16)] * count
        if apart
        else jax.ShapeDtypeStruct((count, BLOCK, width), jnp.bfloat16),
        in_specs=[IN_SMEM] * 3 + [IN_HBM] * (2 * CHIPS + 2),
        out_specs=[IN_HBM] * count if apart else pl.BlockSpec(memory_space=pltpu.VMEM),
        scratch_shapes=[pltpu.VMEM((count, BLOCK, width), jnp.bfloat16)] * apart
        + [
            pltpu.VMEM((count, BLOCK, width), jnp.bfloat16),
            pltpu.VMEM((blocks, kinds - 1, BLOCK, width), jnp.bfloat16),
            pltpu.VMEM((GROUP, -(-blocks // WIDE), tile, WIDE * BLOCK), jnp.float32),
            per_head,
            per_head,
            per_head,
            pltpu.SMEM((blocks + WIDE,), jnp.int32),
            pltpu.SemaphoreType.DMA((6 * CHIPS,)),
        ],
        compiler_params=pltpu.CompilerParams(vmem_limit_bytes=CUT_VMEM),
        cost_estimate=pl.CostEstimate(
            flops=2 * heads * count * blocks * BLOCK * BLOCK * HEAD_DIM,
            bytes_accessed=2 * blocks * kinds * BLOCK * width,
            transcendentals=heads * count * blocks * BLOCK * BLOCK // 2,
        ),
        name="attend",
    )(lengths, pattern, position, *pieces, near_other, far_other)


def per_device(projected_up, projected_down, lengths_up, lengths_down, pattern_up, pattern_down):
    sections, ranks = lax.axis_size("section"), lax.axis_size("ctx")
    blocks, clips = pattern_down.shape[1], lengths_down.shape[1]
    rank = lax.axis_index("ctx").astype(jnp.int32)
    position = jnp.stack([rank // (2 * CHIPS), (rank // 2) % CHIPS, rank % 2])

    def moved(value, flip, steps=0):
        pairs = [
            (section * ranks + rank, (section + steps) % sections * ranks + (rank ^ flip))
            for section in range(sections)
            for rank in range(ranks)
        ]
        return lax.ppermute(value, ("section", "ctx"), pairs)

    def across(value, steps=0):
        return moved(value, 2 * CHIPS, steps)

    def along(pieces):
        return [moved(piece, 2 * offset) if offset else piece for offset, piece in enumerate(pieces)]

    def after(value, *earlier):
        return lax.optimization_barrier((value, *earlier))[0]

    up = projected_up[0].transpose(1, 0, 2)
    down = projected_down[0].transpose(1, 0, 2)

    piece = (*up.shape[:2], up.shape[2] // (2 * CHIPS))

    chips = [[chip * 2 + core for chip in range(2 * CHIPS)] for core in range(2)]

    def spread(pieces):
        return lax.all_to_all(
            pieces, "ctx", split_axis=0, concat_axis=0, axis_index_groups=chips, tiled=True
        )

    up_far = cut_side(up, position, piece, 1)
    both = cut_both(after(up, up_far), down, position, piece, range(CHIPS))
    down_near = cut_each(after(down, both[0]), position, piece, 0)
    up_far = across(up_far)
    both = along(both)
    up_rest = separate(up_far, position)
    both, up_rest, down_near = lax.optimization_barrier((both, up_rest, down_near))

    up_near, down_far = regroup(both, position)
    down_far = across(down_far)
    up_rest = along([None, *up_rest])[1:]
    up_near_other = moved(up_near, 1)
    up_rest, down_near, up_near_other = lax.optimization_barrier(
        (up_rest, down_near, up_near_other)
    )

    down_near = along(down_near)
    up_far = [(up_far, 0)] + [(array, None) for array in up_rest]
    up_near = [(array, 0) for array in both]
    up_far_other = moved(gather(up_far, position), 1)
    up_out = attend(
        up_near + up_far, up_near_other, up_far_other,
        position, lengths_up[0], pattern_up[0], False,
    )
    down_near, down_far, up_out = lax.optimization_barrier((down_near, down_far, up_out))

    up_out = spread(up_out)
    down_near = [(array, None) for array in down_near]
    down_near_other = moved(gather(down_near, position), 1)
    down_far_other = moved(down_far, 1)
    down_far = [(down_far, index) for index in range(CHIPS)]
    down_out = attend(
        down_near + down_far, down_near_other, down_far_other,
        position, lengths_down[0], pattern_down[0], True,
    )

    up_out, down_out = lax.optimization_barrier((up_out, down_out))
    up_out = moved(up_out, 0, 1)
    down_out = [moved(out, 2 * chip, -1) for chip, out in enumerate(down_out)]
    return join(up_out, position)[None], join(down_out, position)[None]


def solution(mesh):
    in_specs = (
        P("section", "ctx", None, None),
        P("section", "ctx", None, None),
        P("section", None),
        P("section", None),
        P("section", None, None),
        P("section", None, None),
    )
    out_specs = (P("section", "ctx", None), P("section", "ctx", None))
    return jax.shard_map(
        per_device, mesh=mesh, in_specs=in_specs, out_specs=out_specs, check_vma=False
    )
```

time: 391 us -> 244 us (0.62)
  Pallas kernels: 0 us -> 80.9 us
  waiting for transfers between devices: 180 us -> 103 us
  local copies, waits for them, and re-layouts: 73.5 us -> 3.34 us
  matrix products: 51.8 us -> 0 us
  other arithmetic: 42 us -> 0.61 us
  starting transfers between devices: 40.6 us -> 53.9 us
    pallas_call x0 -> x11, Pallas kernels: none -> 80.9 us  [the longest x2 50.1 us: attend(): pl.pallas_call(kernel, out_shape=[jax.ShapeDtypeStruct((BLOCK, width), jn...]
    all_to_all x4 -> x1, waiting for transfers between devices: 78.2 us -> 0.01 us  [spread(): lax.all_to_all(pieces, 'ctx', split_axis=0, concat_axis=0, axis_index_gro...]
    dot_general x12 -> x0, matrix products: 51.8 us -> none  [the longest x6 26.4 us: head_attention(): combined = jnp.dot(weights, value_rows, preferred_element_type=jnp.float32)]
    reduce_sum x8 -> x0, other arithmetic: 41.6 us -> none  [the longest x6 41.4 us: head_attention(): totals = jnp.sum(exponentials, axis=1, keepdims=True)]
    ppermute x6 -> x24, starting transfers between devices: 13.2 us -> 46.4 us  [moved(): return lax.ppermute(value, ('section', 'ctx'), pairs)]
    all_to_all x8 -> x0, local copies, waits for them, and re-layouts: 28.9 us -> none  [the longest x2 10 us: per_device(): lax.all_to_all(head_layout(upper[0]), 'ctx', split_axis=3, concat_axis=1,...]
    all_to_all x4 -> x1, starting transfers between devices: 27.4 us -> 7.51 us  [spread(): lax.all_to_all(pieces, 'ctx', split_axis=0, concat_axis=0, axis_index_gro...]
    unnamed x14 -> x32, local copies, waits for them, and re-layouts: 17.6 us -> 3.34 us
  transfers between devices with their start and end apart: 10 -> 25, of which waited for: 5 -> 13; matrix products, arithmetic and copies ran while one was open for 40% -> 0% of each run, Pallas kernels for 0% -> 29%
where the time goes in v1:
time: 244 us; the launch traced here: 243 us
  waiting for transfers between devices  103 us (42%)
  Pallas kernels  80.9 us (33%)
  starting transfers between devices  53.9 us (22%)
  local copies, waits for them, and re-layouts  3.34 us (1%)
    ppermute x24, waiting for transfers between devices, moved(): return lax.ppermute(value, ('section', 'ctx'), pairs)  103 us
    pallas_call x2, Pallas kernels, attend(): pl.pallas_call(kernel, out_shape=[jax.ShapeDtypeStruct((BLOCK, width), jn...  50.1 us
    ppermute x24, starting transfers between devices, moved(): return lax.ppermute(value, ('section', 'ctx'), pairs)  46.4 us
    pallas_call x9, Pallas kernels, copied(): pl.pallas_call(kernel, out_shape=[jax.ShapeDtypeStruct(shape, jnp.bfloat1...  30.8 us
    all_to_all x1, starting transfers between devices, spread(): lax.all_to_all(pieces, 'ctx', split_axis=0, concat_axis=0, axis_index_gro...  7.51 us
  transfers between devices with their start and end apart: 25, of which 13 were waited for; matrix products, arithmetic and copies ran while one was open for 0% of the time, Pallas kernels for 29%

profile of v1, /device:TPU:2, one launch (start us, length us, event | category | flops | bytes accessed | tf_op | source)
XLA Modules:
  0.0 243.3 jit_solution(3296412471738374732)
XLA Ops:
  1.3 3.2 %cut_side.1 = bf16[4,3,128,768]{3,2,1,0:T(8,128)(2,1)} custom-call(s32[3]{0:T(128)} %pad_add_fusion.position.refs_2_, bf16[3,128,6144]{2,1,0:T(8,128)(2,1)} %bitcast.15), custom_call_target="tpu_custom_call" | custom-call | tf_op jit(solution)/shard_map/cut_side/pallas_call | solution.py:62
  4.5 3.3 %collective-permute-start.3 = (bf16[4,3,128,768]{3,2,1,0:T(8,128)(2,1)}, bf16[4,3,128,768]{3,2,1,0:T(8,128)(2,1)S(1)}, u32[]{:S(2)}, u32[]{:S(2)}) collective-permute-start(bf16[4,3,128,768]{3,2,1,0:T(8,128)(2,1)} %cut_side.1), channel_id=1, source_target_pairs={{0,8},{1,9},{2,10},{3,11},{4,12},{5,13},{6,14},{7,15},{8,0},{9,1},... | collective-permute-start | bytes 7077896 | tf_op jit(solution)/shard_map/ppermute | solution.py:397
  7.8 4.9 %cut_both.1 = (bf16[2,3,128,768]{3,2,1,0:T(8,128)(2,1)}, bf16[2,3,128,768]{3,2,1,0:T(8,128)(2,1)}, bf16[2,3,128,768]{3,2,1,0:T(8,128)(2,1)}, bf16[2,3,128,768]{3,2,1,0:T(8,128)(2,1)}) custom-call(s32[3]{0:T(128)} %pad_add_fusion.position.refs_2_, bf16[3,128,6144]{2,1,0:T(8,128)(2,1)} %bitcast.16, bf16[3,128,6144]{2,1,0:T(8,128)(2,1)} %bitcast.17), custom_call_target="tpu_custom_call" | custom-call | tf_op jit(solution)/shard_map/cut_both/pallas_call | solution.py:62
  13.3 2.4 collective-permute-start.1
  16.3 3.2 %cut_each.1 = (bf16[3,128,768]{2,1,0:T(8,128)(2,1)}, bf16[3,128,768]{2,1,0:T(8,128)(2,1)}, bf16[3,128,768]{2,1,0:T(8,128)(2,1)}, bf16[3,128,768]{2,1,0:T(8,128)(2,1)}) custom-call(s32[3]{0:T(128)} %pad_add_fusion.position.refs_2_, bf16[3,128,6144]{2,1,0:T(8,128)(2,1)} %bitcast.18), custom_call_target="tpu_custom_call" | custom-call | tf_op jit(solution)/shard_map/cut_each/pallas_call | solution.py:62
  19.5 39.8 %collective-permute-done.3.refs_0_.refs_7_ = bf16[4,3,128,768]{3,2,1,0:T(8,128)(2,1)S(1)} collective-permute-done((bf16[4,3,128,768]{3,2,1,0:T(8,128)(2,1)}, bf16[4,3,128,768]{3,2,1,0:T(8,128)(2,1)S(1)}, u32[]{:S(2)}, u32[]{:S(2)}) %collective-permute-start.3) | collective-permute-done | bytes 2359328 | tf_op jit(solution)/shard_map/ppermute | solution.py:397
  60.8 3.0 %separate.1 = (bf16[3,128,768]{2,1,0:T(8,128)(2,1)}, bf16[3,128,768]{2,1,0:T(8,128)(2,1)}, bf16[3,128,768]{2,1,0:T(8,128)(2,1)}) custom-call(s32[3]{0:T(128)} %pad_add_fusion.position.refs_2_, bf16[4,3,128,768]{3,2,1,0:T(8,128)(2,1)} %copy-done.1), custom_call_target="tpu_custom_call" | custom-call | tf_op jit(solution)/shard_map/separate/pallas_call | solution.py:62
  63.8 3.1 %collective-permute-done.1.refs_2_.refs_5_ = bf16[2,3,128,768]{3,2,1,0:T(8,128)(2,1)} collective-permute-done((bf16[2,3,128,768]{3,2,1,0:T(8,128)(2,1)}, bf16[2,3,128,768]{3,2,1,0:T(8,128)(2,1)}, u32[]{:S(2)}, u32[]{:S(2)}) %collective-permute-start.1) | collective-permute-done | bytes 1179680 | tf_op jit(solution)/shard_map/ppermute | solution.py:397
  68.2 4.8 %regroup.1 = (bf16[4,3,128,768]{3,2,1,0:T(8,128)(2,1)}, bf16[4,3,128,768]{3,2,1,0:T(8,128)(2,1)}) custom-call(s32[3]{0:T(128)} %pad_add_fusion.position.refs_2_, bf16[2,3,128,768]{3,2,1,0:T(8,128)(2,1)} %get-tuple-element.79.refs_0_.refs_3_, bf16[2,3,128,768]{3,2,1,0:T(8,128)(2,1)} %copy-done.2, ...), custom_call_target="tpu_custom_call" | custom-call | tf_op jit(solution)/shard_map/regroup/pallas_call | solution.py:62
  73.1 3.2 %collective-permute-start.4 = (bf16[3,128,768]{2,1,0:T(8,128)(2,1)}, bf16[3,128,768]{2,1,0:T(8,128)(2,1)S(1)}, u32[]{:S(2)}, u32[]{:S(2)}) collective-permute-start(bf16[3,128,768]{2,1,0:T(8,128)(2,1)} %get-tuple-element.72), channel_id=1, source_target_pairs={{0,2},{1,3},{2,0},{3,1},{4,6},{5,7},{6,4},{7,5},{8,10},{9,11},{10,... | collective-permute-start | bytes 1769480 | tf_op jit(solution)/shard_map/ppermute | solution.py:397
  78.1 12.5 %collective-permute-done.4.refs_1_.refs_8_ = bf16[3,128,768]{2,1,0:T(8,128)(2,1)S(1)} collective-permute-done((bf16[3,128,768]{2,1,0:T(8,128)(2,1)}, bf16[3,128,768]{2,1,0:T(8,128)(2,1)S(1)}, u32[]{:S(2)}, u32[]{:S(2)}) %collective-permute-start.4) | collective-permute-done | bytes 589856 | tf_op jit(solution)/shard_map/ppermute | solution.py:397
  90.6 11.8 %collective-permute-done.5.refs_2_.refs_9_ = bf16[3,128,768]{2,1,0:T(8,128)(2,1)S(1)} collective-permute-done((bf16[3,128,768]{2,1,0:T(8,128)(2,1)}, bf16[3,128,768]{2,1,0:T(8,128)(2,1)S(1)}, u32[]{:S(2)}, u32[]{:S(2)}) %collective-permute-start.5) | collective-permute-done | bytes 589856 | tf_op jit(solution)/shard_map/ppermute | solution.py:397
  102.4 2.2 collective-permute-done.6.refs_3_.refs_10_
  104.6 2.9 %gather.2 = bf16[4,2,128,768]{3,2,1,0:T(8,128)(2,1)} custom-call(s32[3]{0:T(128)} %pad_add_fusion.position.refs_2_, bf16[4,3,128,768]{3,2,1,0:T(8,128)(2,1)} %copy-done.1, bf16[3,128,768]{2,1,0:T(8,128)(2,1)} %copy-done.3, bf16[3,128,768]{2,1,0:T(8,128)(2,1)} %copy-done.4, bf16[3,128,768]{2,1,0:T(8,128)(2,1)} %collective-permute-done.6.refs_3_.refs_10_), custom_call_target="tpu_custom_call" | custom-call | tf_op jit(solution)/shard_map/gather/pallas_call | solution.py:62
  107.6 2.9 %collective-permute-start.8 = (bf16[3,128,768]{2,1,0:T(8,128)(2,1)}, bf16[3,128,768]{2,1,0:T(8,128)(2,1)S(1)}, u32[]{:S(2)}, u32[]{:S(2)}) collective-permute-start(bf16[3,128,768]{2,1,0:T(8,128)(2,1)} %get-tuple-element.85), channel_id=1, source_target_pairs={{0,2},{1,3},{2,0},{3,1},{4,6},{5,7},{6,4},{7,5},{8,10},{9,11},{10,... | collective-permute-start | bytes 1769480 | tf_op jit(solution)/shard_map/ppermute | solution.py:397
  112.7 22.6 %attend.2 = bf16[8,128,768]{2,1,0:T(8,128)(2,1)} custom-call(s32[8]{0:T(128)} %bitcast.23, s32[16,16]{1,0:T(8,128)} %bitcast.22, s32[3]{0:T(128)} %pad_add_fusion.position.refs_2_, bf16[2,3,128,768]{3,2,1,0:T(8,128)(2,1)} %get-tuple-element.79.refs_0_.refs_3_, bf16[2,3,128,768]{3,2,1,0:T(8,128)(2,1)} %copy-done.2, ...), custom_call_target="tpu_custom_call" | custom-call | flops 3221225472 | bytes 9437184 | tf_op jit(solution)/shard_map/attend/pallas_call | solution.py:357
  135.4 3.6 %collective-permute-done.9.refs_2_.refs_5_ = bf16[3,128,768]{2,1,0:T(8,128)(2,1)S(1)} collective-permute-done((bf16[3,128,768]{2,1,0:T(8,128)(2,1)}, bf16[3,128,768]{2,1,0:T(8,128)(2,1)S(1)}, u32[]{:S(2)}, u32[]{:S(2)}) %collective-permute-start.9) | collective-permute-done | bytes 589856 | tf_op jit(solution)/shard_map/ppermute | solution.py:397
  140.5 2.9 %gather.3 = bf16[4,2,128,768]{3,2,1,0:T(8,128)(2,1)} custom-call(s32[3]{0:T(128)} %pad_add_fusion.position.refs_2_, bf16[3,128,768]{2,1,0:T(8,128)(2,1)} %get-tuple-element.94.refs_0_.refs_3_, bf16[3,128,768]{2,1,0:T(8,128)(2,1)} %copy-done.5, bf16[3,128,768]{2,1,0:T(8,128)(2,1)} %copy-done.6, bf16[3,128,768]{2,1,0:T(8,128)(2,1)} %collective-permute-done.10.refs_3_.refs_6_), custom_call_target="tpu_custom_call" | custom-call | tf_op jit(solution)/shard_map/gather/pallas_call | solution.py:62
  144.2 7.5 %all-to-all-start = ((bf16[8,128,768]{2,1,0:T(8,128)(2,1)}), bf16[8,128,768]{2,1,0:T(8,128)(2,1)}, u32[]{:S(2)}, u32[]{:S(2)}) async-start(bf16[8,128,768]{2,1,0:T(8,128)(2,1)} %attend.2), calls=%async_computation | async-start | bytes 3145728 | tf_op jit(solution)/shard_map/all_to_all | solution.py:416
  151.7 27.5 %attend.3 = (bf16[128,768]{1,0:T(8,128)(2,1)}, bf16[128,768]{1,0:T(8,128)(2,1)}, bf16[128,768]{1,0:T(8,128)(2,1)}, bf16[128,768]{1,0:T(8,128)(2,1)}, bf16[128,76...) custom-call(s32[8]{0:T(128)} %bitcast.24, s32[16,16]{1,0:T(8,128)} %bitcast.21, ...), custom_call_target="tpu_custom_call" | custom-call | flops 3221225472 | bytes 9437184 | tf_op jit(solution)/shard_map/attend/pallas_call | solution.py:357
  179.2 2.2 collective-permute-start.15
  181.4 2.2 collective-permute-start.16
  183.6 2.5 %collective-permute-start.18 = (bf16[128,768]{1,0:T(8,128)(2,1)}, bf16[128,768]{1,0:T(8,128)(2,1)S(1)}, u32[]{:S(2)}, u32[]{:S(2)}) collective-permute-start(bf16[128,768]{1,0:T(8,128)(2,1)} %get-tuple-element.110), channel_id=1, source_target_pairs={{0,244},{1,245},{2,246},{3,247},{4,240},{5,241},{6,242},{7,243},{8... | collective-permute-start | bytes 589832 | tf_op jit(solution)/shard_map/ppermute | solution.py:397
  189.2 6.5 %collective-permute-start.20 = (bf16[128,768]{1,0:T(8,128)(2,1)}, bf16[128,768]{1,0:T(8,128)(2,1)S(1)}, u32[]{:S(2)}, u32[]{:S(2)}) collective-permute-start(bf16[128,768]{1,0:T(8,128)(2,1)} %get-tuple-element.112), channel_id=1, source_target_pairs={{0,248},{1,249},{2,250},{3,251},{4,252},{5,253},{6,254},{7,255},{8... | collective-permute-start | bytes 589832 | tf_op jit(solution)/shard_map/ppermute | solution.py:397
  195.8 4.6 %collective-permute-start.21 = (bf16[128,768]{1,0:T(8,128)(2,1)}, bf16[128,768]{1,0:T(8,128)(2,1)S(1)}, u32[]{:S(2)}, u32[]{:S(2)}) collective-permute-start(bf16[128,768]{1,0:T(8,128)(2,1)} %get-tuple-element.113), channel_id=1, source_target_pairs={{0,250},{1,251},{2,248},{3,249},{4,254},{5,255},{6,252},{7,253},{8... | collective-permute-start | bytes 589832 | tf_op jit(solution)/shard_map/ppermute | solution.py:397
  200.4 6.5 %collective-permute-start.22 = (bf16[128,768]{1,0:T(8,128)(2,1)}, bf16[128,768]{1,0:T(8,128)(2,1)S(1)}, u32[]{:S(2)}, u32[]{:S(2)}) collective-permute-start(bf16[128,768]{1,0:T(8,128)(2,1)} %get-tuple-element.114), channel_id=1, source_target_pairs={{0,252},{1,253},{2,254},{3,255},{4,248},{5,249},{6,250},{7,251},{8... | collective-permute-start | bytes 589832 | tf_op jit(solution)/shard_map/ppermute | solution.py:397
  208.8 2.5 %collective-permute-done.20.refs_4_ = bf16[128,768]{1,0:T(8,128)(2,1)S(1)} collective-permute-done((bf16[128,768]{1,0:T(8,128)(2,1)}, bf16[128,768]{1,0:T(8,128)(2,1)S(1)}, u32[]{:S(2)}, u32[]{:S(2)}) %collective-permute-start.20) | collective-permute-done | bytes 196640 | tf_op jit(solution)/shard_map/ppermute | solution.py:397
  211.3 13.9 %collective-permute-done.21.refs_5_ = bf16[128,768]{1,0:T(8,128)(2,1)S(1)} collective-permute-done((bf16[128,768]{1,0:T(8,128)(2,1)}, bf16[128,768]{1,0:T(8,128)(2,1)S(1)}, u32[]{:S(2)}, u32[]{:S(2)}) %collective-permute-start.21) | collective-permute-done | bytes 196640 | tf_op jit(solution)/shard_map/ppermute | solution.py:397
  225.2 3.9 %collective-permute-done.22.refs_6_ = bf16[128,768]{1,0:T(8,128)(2,1)S(1)} collective-permute-done((bf16[128,768]{1,0:T(8,128)(2,1)}, bf16[128,768]{1,0:T(8,128)(2,1)S(1)}, u32[]{:S(2)}, u32[]{:S(2)}) %collective-permute-start.22) | collective-permute-done | bytes 196640 | tf_op jit(solution)/shard_map/ppermute | solution.py:397
  229.2 6.1 %collective-permute-done.23.refs_7_ = bf16[128,768]{1,0:T(8,128)(2,1)S(1)} collective-permute-done((bf16[128,768]{1,0:T(8,128)(2,1)}, bf16[128,768]{1,0:T(8,128)(2,1)S(1)}, u32[]{:S(2)}, u32[]{:S(2)}) %collective-permute-start.23) | collective-permute-done | bytes 196640 | tf_op jit(solution)/shard_map/ppermute | solution.py:397
  236.0 3.0 %join.3 = bf16[128,6144]{1,0:T(8,128)(2,1)} custom-call(s32[3]{0:T(128)} %pad_add_fusion.position.refs_2_, bf16[128,768]{1,0:T(8,128)(2,1)} %copy-done.8, bf16[128,768]{1,0:T(8,128)(2,1)} %copy-done.9, bf16[128,768]{1,0:T(8,128)(2,1)} %copy-done.10, bf16[128,768]{1,0:T(8,128)(2,1)} %copy-done.11, bf16[128,768]{1,0:T(8,128)(2,1)} %copy-done.12, ...), custom_call_target="tpu_custom_call" | custom-call | tf_op jit(solution)/shard_map/join/pallas_call | solution.py:62
  240.1 3.0 %join.2 = bf16[128,6144]{1,0:T(8,128)(2,1)} custom-call(s32[3]{0:T(128)} %pad_add_fusion.position.refs_2_, bf16[8,128,768]{2,1,0:T(8,128)(2,1)} %copy-done.7), custom_call_target="tpu_custom_call" | custom-call | tf_op jit(solution)/shard_map/join/pallas_call | solution.py:62
  (62 shorter events, 18.1 us)
Async XLA Ops:
  4.5 54.8 %collective-permute-start.3 = (bf16[4,3,128,768]{3,2,1,0:T(8,128)(2,1)}, bf16[4,3,128,768]{3,2,1,0:T(8,128)(2,1)S(1)}, u32[]{:S(2)}, u32[]{:S(2)}) collective-permute-start(bf16[4,3,128,768]{3,2,1,0:T(8,128)(2,1)} %cut_side.1), channel_id=1, source_target_pairs={{0,8},{1,9},{2,10},{3,11},{4,12},{5,13},{6,14},{7,15},{8,0},{9,1},... | collective-permute-start | bytes 7077896 | tf_op jit(solution)/shard_map/ppermute | solution.py:397
  12.7 51.1 %collective-permute-start = (bf16[2,3,128,768]{3,2,1,0:T(8,128)(2,1)}, bf16[2,3,128,768]{3,2,1,0:T(8,128)(2,1)S(1)}, u32[]{:S(2)}, u32[]{:S(2)}) collective-permute-start(bf16[2,3,128,768]{3,2,1,0:T(8,128)(2,1)} %get-tuple-element.61), channel_id=1, source_target_pairs={{0,2},{1,3},{2,0},{3,1},{4,6},{5,7},{6,4},{7,5},{8,10},{9,11},{10,... | collective-permute-start | bytes 3538952 | tf_op jit(solution)/shard_map/ppermute | solution.py:397
  13.3 53.5 %collective-permute-start.1 = (bf16[2,3,128,768]{3,2,1,0:T(8,128)(2,1)}, bf16[2,3,128,768]{3,2,1,0:T(8,128)(2,1)}, u32[]{:S(2)}, u32[]{:S(2)}) collective-permute-start(bf16[2,3,128,768]{3,2,1,0:T(8,128)(2,1)} %get-tuple-element.62), channel_id=1, source_target_pairs={{0,4},{1,5},{2,6},{3,7},{4,0},{5,1},{6,2},{7,3},{8,12},{9,13},{10,... | collective-permute-start | bytes 3538952 | tf_op jit(solution)/shard_map/ppermute | solution.py:397
  15.7 52.5 %collective-permute-start.2 = (bf16[2,3,128,768]{3,2,1,0:T(8,128)(2,1)}, bf16[2,3,128,768]{3,2,1,0:T(8,128)(2,1)}, u32[]{:S(2)}, u32[]{:S(2)}) collective-permute-start(bf16[2,3,128,768]{3,2,1,0:T(8,128)(2,1)} %get-tuple-element.63), channel_id=1, source_target_pairs={{0,6},{1,7},{2,4},{3,5},{4,2},{5,3},{6,0},{7,1},{8,14},{9,15},{10,... | collective-permute-start | bytes 3538952 | tf_op jit(solution)/shard_map/ppermute | solution.py:397
  73.0 31.6 %collective-permute-start.7 = (bf16[4,3,128,768]{3,2,1,0:T(8,128)(2,1)}, bf16[4,3,128,768]{3,2,1,0:T(8,128)(2,1)}, u32[]{:S(2)}, u32[]{:S(2)}) collective-permute-start(bf16[4,3,128,768]{3,2,1,0:T(8,128)(2,1)} %get-tuple-element.83), channel_id=1, source_target_pairs={{0,1},{1,0},{2,3},{3,2},{4,5},{5,4},{6,7},{7,6},{8,9},{9,8},{10,11... | collective-permute-start | bytes 7077896 | tf_op jit(solution)/shard_map/ppermute | solution.py:397
  73.1 17.5 %collective-permute-start.4 = (bf16[3,128,768]{2,1,0:T(8,128)(2,1)}, bf16[3,128,768]{2,1,0:T(8,128)(2,1)S(1)}, u32[]{:S(2)}, u32[]{:S(2)}) collective-permute-start(bf16[3,128,768]{2,1,0:T(8,128)(2,1)} %get-tuple-element.72), channel_id=1, source_target_pairs={{0,2},{1,3},{2,0},{3,1},{4,6},{5,7},{6,4},{7,5},{8,10},{9,11},{10,... | collective-permute-start | bytes 1769480 | tf_op jit(solution)/shard_map/ppermute | solution.py:397
  76.3 26.2 %collective-permute-start.5 = (bf16[3,128,768]{2,1,0:T(8,128)(2,1)}, bf16[3,128,768]{2,1,0:T(8,128)(2,1)S(1)}, u32[]{:S(2)}, u32[]{:S(2)}) collective-permute-start(bf16[3,128,768]{2,1,0:T(8,128)(2,1)} %get-tuple-element.73), channel_id=1, source_target_pairs={{0,4},{1,5},{2,6},{3,7},{4,0},{5,1},{6,2},{7,3},{8,12},{9,13},{10,... | collective-permute-start | bytes 1769480 | tf_op jit(solution)/shard_map/ppermute | solution.py:397
  76.3 28.3 %collective-permute-start.6 = (bf16[3,128,768]{2,1,0:T(8,128)(2,1)}, bf16[3,128,768]{2,1,0:T(8,128)(2,1)}, u32[]{:S(2)}, u32[]{:S(2)}) collective-permute-start(bf16[3,128,768]{2,1,0:T(8,128)(2,1)} %get-tuple-element.74), channel_id=1, source_target_pairs={{0,6},{1,7},{2,4},{3,5},{4,2},{5,3},{6,0},{7,1},{8,14},{9,15},{10,... | collective-permute-start | bytes 1769480 | tf_op jit(solution)/shard_map/ppermute | solution.py:397
  77.8 57.5 %collective-permute-start.11 = (bf16[4,3,128,768]{3,2,1,0:T(8,128)(2,1)}, bf16[4,3,128,768]{3,2,1,0:T(8,128)(2,1)S(1)}, u32[]{:S(2)}, u32[]{:S(2)}) collective-permute-start(bf16[4,3,128,768]{3,2,1,0:T(8,128)(2,1)} %get-tuple-element.88), channel_id=1, source_target_pairs={{0,8},{1,9},{2,10},{3,11},{4,12},{5,13},{6,14},{7,15},{8,0},{9,1},... | collective-permute-start | bytes 7077896 | tf_op jit(solution)/shard_map/ppermute | solution.py:397
  90.6 14.0 %copy-start.3 = (bf16[3,128,768]{2,1,0:T(8,128)(2,1)}, bf16[3,128,768]{2,1,0:T(8,128)(2,1)S(1)}, u32[]{:S(2)}) copy-start(bf16[3,128,768]{2,1,0:T(8,128)(2,1)S(1)} %collective-permute-done.4.refs_1_.refs_8_) | copy-start | bytes 1769476
  107.5 5.2 %collective-permute-start.12 = (bf16[4,2,128,768]{3,2,1,0:T(8,128)(2,1)}, bf16[4,2,128,768]{3,2,1,0:T(8,128)(2,1)}, u32[]{:S(2)}, u32[]{:S(2)}) collective-permute-start(bf16[4,2,128,768]{3,2,1,0:T(8,128)(2,1)} %gather.2), channel_id=1, source_target_pairs={{0,1},{1,0},{2,3},{3,2},{4,5},{5,4},{6,7},{7,6},{8,9},{9,8},{10,11... | collective-permute-start | bytes 4718600 | tf_op jit(solution)/shard_map/ppermute | solution.py:397
  107.6 27.8 %collective-permute-start.8 = (bf16[3,128,768]{2,1,0:T(8,128)(2,1)}, bf16[3,128,768]{2,1,0:T(8,128)(2,1)S(1)}, u32[]{:S(2)}, u32[]{:S(2)}) collective-permute-start(bf16[3,128,768]{2,1,0:T(8,128)(2,1)} %get-tuple-element.85), channel_id=1, source_target_pairs={{0,2},{1,3},{2,0},{3,1},{4,6},{5,7},{6,4},{7,5},{8,10},{9,11},{10,... | collective-permute-start | bytes 1769480 | tf_op jit(solution)/shard_map/ppermute | solution.py:397
  110.5 28.5 %collective-permute-start.9 = (bf16[3,128,768]{2,1,0:T(8,128)(2,1)}, bf16[3,128,768]{2,1,0:T(8,128)(2,1)S(1)}, u32[]{:S(2)}, u32[]{:S(2)}) collective-permute-start(bf16[3,128,768]{2,1,0:T(8,128)(2,1)} %get-tuple-element.86), channel_id=1, source_target_pairs={{0,4},{1,5},{2,6},{3,7},{4,0},{5,1},{6,2},{7,3},{8,12},{9,13},{10,... | collective-permute-start | bytes 1769480 | tf_op jit(solution)/shard_map/ppermute | solution.py:397
  112.2 28.2 %collective-permute-start.10 = (bf16[3,128,768]{2,1,0:T(8,128)(2,1)}, bf16[3,128,768]{2,1,0:T(8,128)(2,1)}, u32[]{:S(2)}, u32[]{:S(2)}) collective-permute-start(bf16[3,128,768]{2,1,0:T(8,128)(2,1)} %get-tuple-element.87), channel_id=1, source_target_pairs={{0,6},{1,7},{2,4},{3,5},{4,2},{5,3},{6,0},{7,1},{8,14},{9,15},{10,... | collective-permute-start | bytes 1769480 | tf_op jit(solution)/shard_map/ppermute | solution.py:397
  140.4 11.3 %collective-permute-start.14 = (bf16[4,3,128,768]{3,2,1,0:T(8,128)(2,1)S(1)}, bf16[4,3,128,768]{3,2,1,0:T(8,128)(2,1)}, u32[]{:S(2)}, u32[]{:S(2)}) collective-permute-start(bf16[4,3,128,768]{3,2,1,0:T(8,128)(2,1)S(1)} %collective-permute-done.11.refs_7_.refs_8_.refs_9_.refs_10_), channel_id=1, source_target_pairs={{0,1},{1,0},{2,3},{3,2},{4,5},{5,4},{6,7},{7,6},{8,9},{9,8},{10,11... | collective-permute-start | bytes 7077896 | tf_op jit(solution)/shard_map/ppermute | solution.py:397
  143.3 8.4 %collective-permute-start.13 = (bf16[4,2,128,768]{3,2,1,0:T(8,128)(2,1)}, bf16[4,2,128,768]{3,2,1,0:T(8,128)(2,1)}, u32[]{:S(2)}, u32[]{:S(2)}) collective-permute-start(bf16[4,2,128,768]{3,2,1,0:T(8,128)(2,1)} %gather.3), channel_id=1, source_target_pairs={{0,1},{1,0},{2,3},{3,2},{4,5},{5,4},{6,7},{7,6},{8,9},{9,8},{10,11... | collective-permute-start | bytes 4718600 | tf_op jit(solution)/shard_map/ppermute | solution.py:397
  144.2 35.0 %all-to-all-start = ((bf16[8,128,768]{2,1,0:T(8,128)(2,1)}), bf16[8,128,768]{2,1,0:T(8,128)(2,1)}, u32[]{:S(2)}, u32[]{:S(2)}) async-start(bf16[8,128,768]{2,1,0:T(8,128)(2,1)} %attend.2), calls=%async_computation | async-start | bytes 3145728 | tf_op jit(solution)/shard_map/all_to_all | solution.py:416
  179.2 59.7 %collective-permute-start.15 = (bf16[8,128,768]{2,1,0:T(8,128)(2,1)}, bf16[8,128,768]{2,1,0:T(8,128)(2,1)S(1)}, u32[]{:S(2)}, u32[]{:S(2)}) collective-permute-start(bf16[8,128,768]{2,1,0:T(8,128)(2,1)} %all-to-all-done), channel_id=1, source_target_pairs={{0,16},{1,17},{2,18},{3,19},{4,20},{5,21},{6,22},{7,23},{8,24},{9,... | collective-permute-start | bytes 4718600 | tf_op jit(solution)/shard_map/ppermute | solution.py:397
  181.4 7.8 %collective-permute-start.16 = (bf16[128,768]{1,0:T(8,128)(2,1)}, bf16[128,768]{1,0:T(8,128)(2,1)S(1)}, u32[]{:S(2)}, u32[]{:S(2)}) collective-permute-start(bf16[128,768]{1,0:T(8,128)(2,1)} %get-tuple-element.108), channel_id=1, source_target_pairs={{0,240},{1,241},{2,242},{3,243},{4,244},{5,245},{6,246},{7,247},{8... | collective-permute-start | bytes 589832 | tf_op jit(solution)/shard_map/ppermute | solution.py:397
  183.6 12.1 %collective-permute-start.17 = (bf16[128,768]{1,0:T(8,128)(2,1)}, bf16[128,768]{1,0:T(8,128)(2,1)S(1)}, u32[]{:S(2)}, u32[]{:S(2)}) collective-permute-start(bf16[128,768]{1,0:T(8,128)(2,1)} %get-tuple-element.109), channel_id=1, source_target_pairs={{0,242},{1,243},{2,240},{3,241},{4,246},{5,247},{6,244},{7,245},{8... | collective-permute-start | bytes 589832 | tf_op jit(solution)/shard_map/ppermute | solution.py:397
  183.6 16.7 %collective-permute-start.18 = (bf16[128,768]{1,0:T(8,128)(2,1)}, bf16[128,768]{1,0:T(8,128)(2,1)S(1)}, u32[]{:S(2)}, u32[]{:S(2)}) collective-permute-start(bf16[128,768]{1,0:T(8,128)(2,1)} %get-tuple-element.110), channel_id=1, source_target_pairs={{0,244},{1,245},{2,246},{3,247},{4,240},{5,241},{6,242},{7,243},{8... | collective-permute-start | bytes 589832 | tf_op jit(solution)/shard_map/ppermute | solution.py:397
  186.2 20.7 %collective-permute-start.19 = (bf16[128,768]{1,0:T(8,128)(2,1)}, bf16[128,768]{1,0:T(8,128)(2,1)S(1)}, u32[]{:S(2)}, u32[]{:S(2)}) collective-permute-start(bf16[128,768]{1,0:T(8,128)(2,1)} %get-tuple-element.111), channel_id=1, source_target_pairs={{0,246},{1,247},{2,244},{3,245},{4,242},{5,243},{6,240},{7,241},{8... | collective-permute-start | bytes 589832 | tf_op jit(solution)/shard_map/ppermute | solution.py:397
  189.2 46.0 %copy-start.8 = (bf16[128,768]{1,0:T(8,128)(2,1)}, bf16[128,768]{1,0:T(8,128)(2,1)S(1)}, u32[]{:S(2)}) copy-start(bf16[128,768]{1,0:T(8,128)(2,1)S(1)} %collective-permute-done.16.refs_0_) | copy-start | bytes 589828
  189.2 22.1 %collective-permute-start.20 = (bf16[128,768]{1,0:T(8,128)(2,1)}, bf16[128,768]{1,0:T(8,128)(2,1)S(1)}, u32[]{:S(2)}, u32[]{:S(2)}) collective-permute-start(bf16[128,768]{1,0:T(8,128)(2,1)} %get-tuple-element.112), channel_id=1, source_target_pairs={{0,248},{1,249},{2,250},{3,251},{4,252},{5,253},{6,254},{7,255},{8... | collective-permute-start | bytes 589832 | tf_op jit(solution)/shard_map/ppermute | solution.py:397
  195.8 39.5 %copy-start.9 = (bf16[128,768]{1,0:T(8,128)(2,1)}, bf16[128,768]{1,0:T(8,128)(2,1)S(1)}, u32[]{:S(2)}) copy-start(bf16[128,768]{1,0:T(8,128)(2,1)S(1)} %collective-permute-done.17.refs_1_) | copy-start | bytes 589828
  195.8 29.5 %collective-permute-start.21 = (bf16[128,768]{1,0:T(8,128)(2,1)}, bf16[128,768]{1,0:T(8,128)(2,1)S(1)}, u32[]{:S(2)}, u32[]{:S(2)}) collective-permute-start(bf16[128,768]{1,0:T(8,128)(2,1)} %get-tuple-element.113), channel_id=1, source_target_pairs={{0,250},{1,251},{2,248},{3,249},{4,254},{5,255},{6,252},{7,253},{8... | collective-permute-start | bytes 589832 | tf_op jit(solution)/shard_map/ppermute | solution.py:397
  200.4 34.9 %copy-start.10 = (bf16[128,768]{1,0:T(8,128)(2,1)}, bf16[128,768]{1,0:T(8,128)(2,1)S(1)}, u32[]{:S(2)}) copy-start(bf16[128,768]{1,0:T(8,128)(2,1)S(1)} %collective-permute-done.18.refs_2_) | copy-start | bytes 589828
  200.4 28.8 %collective-permute-start.22 = (bf16[128,768]{1,0:T(8,128)(2,1)}, bf16[128,768]{1,0:T(8,128)(2,1)S(1)}, u32[]{:S(2)}, u32[]{:S(2)}) collective-permute-start(bf16[128,768]{1,0:T(8,128)(2,1)} %get-tuple-element.114), channel_id=1, source_target_pairs={{0,252},{1,253},{2,254},{3,255},{4,248},{5,249},{6,250},{7,251},{8... | collective-permute-start | bytes 589832 | tf_op jit(solution)/shard_map/ppermute | solution.py:397
  206.8 28.4 %copy-start.11 = (bf16[128,768]{1,0:T(8,128)(2,1)}, bf16[128,768]{1,0:T(8,128)(2,1)S(1)}, u32[]{:S(2)}) copy-start(bf16[128,768]{1,0:T(8,128)(2,1)S(1)} %collective-permute-done.19.refs_3_) | copy-start | bytes 589828
  206.9 28.4 %collective-permute-start.23 = (bf16[128,768]{1,0:T(8,128)(2,1)}, bf16[128,768]{1,0:T(8,128)(2,1)S(1)}, u32[]{:S(2)}, u32[]{:S(2)}) collective-permute-start(bf16[128,768]{1,0:T(8,128)(2,1)} %get-tuple-element.115), channel_id=1, source_target_pairs={{0,254},{1,255},{2,252},{3,253},{4,250},{5,251},{6,248},{7,249},{8... | collective-permute-start | bytes 589832 | tf_op jit(solution)/shard_map/ppermute | solution.py:397
  211.3 23.9 %copy-start.12 = (bf16[128,768]{1,0:T(8,128)(2,1)}, bf16[128,768]{1,0:T(8,128)(2,1)S(1)}, u32[]{:S(2)}) copy-start(bf16[128,768]{1,0:T(8,128)(2,1)S(1)} %collective-permute-done.20.refs_4_) | copy-start | bytes 589828
  225.2 10.0 %copy-start.13 = (bf16[128,768]{1,0:T(8,128)(2,1)}, bf16[128,768]{1,0:T(8,128)(2,1)S(1)}, u32[]{:S(2)}) copy-start(bf16[128,768]{1,0:T(8,128)(2,1)S(1)} %collective-permute-done.21.refs_5_) | copy-start | bytes 589828
  (9 other events, 30.6 us)

commit v2 on v1

--- a/solution.py
+++ b/solution.py
@@ -12,7 +12,7 @@
 BLOCK = 128
 TALL = 2
 WIDE = 4
-GROUP = 3
+GROUP = 6
 CHIPS = 4
 CUT_VMEM = 60 * 1024 * 1024
 
@@ -181,9 +181,10 @@
     return copied(plan, inputs, [shape], position, "join", (tokens, width))[0]
 
 
-def attend_kernel(places, apart, lengths, pattern, position, *refs):
+def attend_kernel(places, side, lengths, pattern, position, *refs):
     pieces = refs[: 2 * CHIPS]
     near_other, far_other = refs[2 * CHIPS : 2 * CHIPS + 2]
+    apart = side is not None
     scratch = refs[-9:] if apart else refs[-8:]
     asked, held, scores, largest, totals, combined, listed, arrived = scratch[-8:]
     outs = refs[2 * CHIPS + 2 : -len(scratch)]
@@ -200,8 +201,12 @@
 
     copies = []
     for piece in range(2 * CHIPS):
-        chip = block_of(piece, core) // 2
-        copies.append((part(pieces[piece], places[piece]).at[0], asked.at[chip]))
+        if apart:
+            slot = piece % CHIPS
+        else:
+            slot = block_of(piece, core) // 2
+        if side in (None, piece // CHIPS):
+            copies.append((part(pieces[piece], places[piece]).at[0], asked.at[slot]))
         mine = part(pieces[piece], places[piece]).at[pl.ds(1, 2)]
         copies.append((mine, held.at[block_of(piece, core)]))
         other = (near_other if piece < CHIPS else far_other).at[piece % CHIPS]
@@ -231,8 +236,14 @@
         copy.wait()
 
     def rows(step, _):
-        own = [(step * TALL + row) * 2 + core for row in range(TALL)]
-        first, last = own[0] * BLOCK, own[-1] * BLOCK + BLOCK - 1
+        if apart:
+            own = [block_of(side * CHIPS + step * TALL + row, core) for row in range(TALL)]
+        else:
+            own = [(step * TALL + row) * 2 + core for row in range(TALL)]
+        first, last = own[0], own[0]
+        for block in own[1:]:
+            first, last = jnp.minimum(first, block), jnp.maximum(last, block)
+        first, last = first * BLOCK, last * BLOCK + BLOCK - 1
         low, high = jnp.int32(0), bounds[-1]
         for bound in bounds:
             low = jnp.where(bound <= first, bound, low)
@@ -331,10 +342,10 @@
         lax.fori_loop(0, out_ref.shape[2] // (group_heads * HEAD_DIM), heads, 0)
         return 0
 
-    lax.fori_loop(0, 2 * CHIPS // TALL, rows, 0)
+    lax.fori_loop(0, out_ref.shape[0] // TALL, rows, 0)
     if apart:
         copies = [
-            pltpu.make_async_copy(out_ref.at[block_of(slot, core) // 2], out, arrived.at[slot])
+            pltpu.make_async_copy(out_ref.at[slot], out, arrived.at[slot])
             for slot, out in enumerate(outs)
         ]
         for copy in copies:
@@ -343,16 +354,17 @@
             copy.wait()
 
 
-def attend(pieces, near_other, far_other, position, lengths, pattern, apart):
+def attend(pieces, near_other, far_other, position, lengths, pattern, side=None):
     places = [where for _, where in pieces]
     pieces = [array for array, _ in pieces]
     kinds, _, width = pieces[0].shape[-3:]
     blocks, tile = 4 * CHIPS, TALL * BLOCK
-    heads, count = width // HEAD_DIM, 2 * CHIPS
+    heads, apart = width // HEAD_DIM, side is not None
+    count = CHIPS if apart else 2 * CHIPS
     per_head = pltpu.VMEM((GROUP, tile, BLOCK), jnp.float32)
 
     def kernel(*refs):
-        attend_kernel(places, apart, *refs)
+        attend_kernel(places, side, *refs)
 
     return pl.pallas_call(
         kernel,
@@ -384,7 +396,6 @@
 
 def per_device(projected_up, projected_down, lengths_up, lengths_down, pattern_up, pattern_down):
     sections, ranks = lax.axis_size("section"), lax.axis_size("ctx")
-    blocks, clips = pattern_down.shape[1], lengths_down.shape[1]
     rank = lax.axis_index("ctx").astype(jnp.int32)
     position = jnp.stack([rank // (2 * CHIPS), (rank // 2) % CHIPS, rank % 2])
 
@@ -439,7 +450,7 @@
     up_far_other = moved(gather(up_far, position), 1)
     up_out = attend(
         up_near + up_far, up_near_other, up_far_other,
-        position, lengths_up[0], pattern_up[0], False,
+        position, lengths_up[0], pattern_up[0],
     )
     down_near, down_far, up_out = lax.optimization_barrier((down_near, down_far, up_out))
 
@@ -448,15 +459,16 @@
     down_near_other = moved(gather(down_near, position), 1)
     down_far_other = moved(down_far, 1)
     down_far = [(down_far, index) for index in range(CHIPS)]
-    down_out = attend(
-        down_near + down_far, down_near_other, down_far_other,
-        position, lengths_down[0], pattern_down[0], True,
-    )
-
-    up_out, down_out = lax.optimization_barrier((up_out, down_out))
+    args = (down_near + down_far, down_near_other, down_far_other)
+    clips = (lengths_down[0], pattern_down[0])
+
+    far_out = attend(*args, position, *clips, 1)
+    near_out = attend(*args, after(position, far_out[0]), *clips, 0)
+    far_out = [moved(out, 2 * CHIPS + 2 * chip, -1) for chip, out in enumerate(far_out)]
+    near_out, far_out, up_out = lax.optimization_barrier((near_out, far_out, up_out))
     up_out = moved(up_out, 0, 1)
-    down_out = [moved(out, 2 * chip, -1) for chip, out in enumerate(down_out)]
-    return join(up_out, position)[None], join(down_out, position)[None]
+    near_out = [moved(out, 2 * chip, -1) for chip, out in enumerate(near_out)]
+    return join(up_out, position)[None], join(near_out + far_out, position)[None]
 
 
 def solution(mesh):

time: 244 us -> 238 us (0.975)
  Pallas kernels: 80.9 us -> 77.8 us
  starting transfers between devices: 53.9 us -> 51.1 us
    ppermute x24, starting transfers between devices: 46.4 us -> 43.4 us  [moved(): return lax.ppermute(value, ('section', 'ctx'), pairs)]
    pallas_call x2 -> x3, Pallas kernels: 50.1 us -> 47.1 us  [attend(): pl.pallas_call(kernel, out_shape=[jax.ShapeDtypeStruct((BLOCK, width), jn...]
    ppermute x24, waiting for transfers between devices: 103 us -> 101 us  [moved(): return lax.ppermute(value, ('section', 'ctx'), pairs)]
  transfers between devices with their start and end apart: 25 -> 25, of which waited for: 13 -> 13; matrix products, arithmetic and copies ran while one was open for 0% -> 0% of each run, Pallas kernels for 29% -> 28%
where the time goes in v2:
time: 238 us; the launch traced here: 235 us
  waiting for transfers between devices  101 us (42%)
  Pallas kernels  77.8 us (33%)
  starting transfers between devices  51.1 us (21%)
  local copies, waits for them, and re-layouts  3.34 us (1%)
    ppermute x24, waiting for transfers between devices, moved(): return lax.ppermute(value, ('section', 'ctx'), pairs)  101 us
    pallas_call x3, Pallas kernels, attend(): pl.pallas_call(kernel, out_shape=[jax.ShapeDtypeStruct((BLOCK, width), jn...  47.1 us
    ppermute x24, starting transfers between devices, moved(): return lax.ppermute(value, ('section', 'ctx'), pairs)  43.4 us
    pallas_call x9, Pallas kernels, copied(): pl.pallas_call(kernel, out_shape=[jax.ShapeDtypeStruct(shape, jnp.bfloat1...  30.7 us
    all_to_all x1, starting transfers between devices, spread(): lax.all_to_all(pieces, 'ctx', split_axis=0, concat_axis=0, axis_index_gro...  7.76 us
  transfers between devices with their start and end apart: 25, of which 13 were waited for; matrix products, arithmetic and copies ran while one was open for 0% of the time, Pallas kernels for 28%

profile of v2, /device:TPU:2, one launch (start us, length us, event | category | flops | bytes accessed | tf_op | source)
XLA Modules:
  0.0 235.0 jit_solution(15063602055828936145)
XLA Ops:
  1.3 3.2 %cut_side.1 = bf16[4,3,128,768]{3,2,1,0:T(8,128)(2,1)} custom-call(s32[3]{0:T(128)} %pad_add_fusion.position.refs_2_, bf16[3,128,6144]{2,1,0:T(8,128)(2,1)} %bitcast.15), custom_call_target="tpu_custom_call" | custom-call | tf_op jit(solution)/shard_map/cut_side/pallas_call | solution.py:62
  4.6 3.3 %collective-permute-start.3 = (bf16[4,3,128,768]{3,2,1,0:T(8,128)(2,1)}, bf16[4,3,128,768]{3,2,1,0:T(8,128)(2,1)S(1)}, u32[]{:S(2)}, u32[]{:S(2)}) collective-permute-start(bf16[4,3,128,768]{3,2,1,0:T(8,128)(2,1)} %cut_side.1), channel_id=1, source_target_pairs={{0,8},{1,9},{2,10},{3,11},{4,12},{5,13},{6,14},{7,15},{8,0},{9,1},... | collective-permute-start | bytes 7077896 | tf_op jit(solution)/shard_map/ppermute | solution.py:408
  7.8 4.9 %cut_both.1 = (bf16[2,3,128,768]{3,2,1,0:T(8,128)(2,1)}, bf16[2,3,128,768]{3,2,1,0:T(8,128)(2,1)}, bf16[2,3,128,768]{3,2,1,0:T(8,128)(2,1)}, bf16[2,3,128,768]{3,2,1,0:T(8,128)(2,1)}) custom-call(s32[3]{0:T(128)} %pad_add_fusion.position.refs_2_, bf16[3,128,6144]{2,1,0:T(8,128)(2,1)} %bitcast.16, bf16[3,128,6144]{2,1,0:T(8,128)(2,1)} %bitcast.17), custom_call_target="tpu_custom_call" | custom-call | tf_op jit(solution)/shard_map/cut_both/pallas_call | solution.py:62
  13.4 2.4 %collective-permute-start.1 = (bf16[2,3,128,768]{3,2,1,0:T(8,128)(2,1)}, bf16[2,3,128,768]{3,2,1,0:T(8,128)(2,1)}, u32[]{:S(2)}, u32[]{:S(2)}) collective-permute-start(bf16[2,3,128,768]{3,2,1,0:T(8,128)(2,1)} %get-tuple-element.63), channel_id=1, source_target_pairs={{0,4},{1,5},{2,6},{3,7},{4,0},{5,1},{6,2},{7,3},{8,12},{9,13},{10,... | collective-permute-start | bytes 3538952 | tf_op jit(solution)/shard_map/ppermute | solution.py:408
  16.3 3.2 %cut_each.1 = (bf16[3,128,768]{2,1,0:T(8,128)(2,1)}, bf16[3,128,768]{2,1,0:T(8,128)(2,1)}, bf16[3,128,768]{2,1,0:T(8,128)(2,1)}, bf16[3,128,768]{2,1,0:T(8,128)(2,1)}) custom-call(s32[3]{0:T(128)} %pad_add_fusion.position.refs_2_, bf16[3,128,6144]{2,1,0:T(8,128)(2,1)} %bitcast.18), custom_call_target="tpu_custom_call" | custom-call | tf_op jit(solution)/shard_map/cut_each/pallas_call | solution.py:62
  19.5 39.8 %collective-permute-done.3.refs_0_.refs_7_ = bf16[4,3,128,768]{3,2,1,0:T(8,128)(2,1)S(1)} collective-permute-done((bf16[4,3,128,768]{3,2,1,0:T(8,128)(2,1)}, bf16[4,3,128,768]{3,2,1,0:T(8,128)(2,1)S(1)}, u32[]{:S(2)}, u32[]{:S(2)}) %collective-permute-start.3) | collective-permute-done | bytes 2359328 | tf_op jit(solution)/shard_map/ppermute | solution.py:408
  60.8 3.0 %separate.1 = (bf16[3,128,768]{2,1,0:T(8,128)(2,1)}, bf16[3,128,768]{2,1,0:T(8,128)(2,1)}, bf16[3,128,768]{2,1,0:T(8,128)(2,1)}) custom-call(s32[3]{0:T(128)} %pad_add_fusion.position.refs_2_, bf16[4,3,128,768]{3,2,1,0:T(8,128)(2,1)} %copy-done.1), custom_call_target="tpu_custom_call" | custom-call | tf_op jit(solution)/shard_map/separate/pallas_call | solution.py:62
  63.8 3.1 %collective-permute-done.1.refs_2_.refs_5_ = bf16[2,3,128,768]{3,2,1,0:T(8,128)(2,1)} collective-permute-done((bf16[2,3,128,768]{3,2,1,0:T(8,128)(2,1)}, bf16[2,3,128,768]{3,2,1,0:T(8,128)(2,1)}, u32[]{:S(2)}, u32[]{:S(2)}) %collective-permute-start.1) | collective-permute-done | bytes 1179680 | tf_op jit(solution)/shard_map/ppermute | solution.py:408
  68.2 4.8 %regroup.1 = (bf16[4,3,128,768]{3,2,1,0:T(8,128)(2,1)}, bf16[4,3,128,768]{3,2,1,0:T(8,128)(2,1)}) custom-call(s32[3]{0:T(128)} %pad_add_fusion.position.refs_2_, bf16[2,3,128,768]{3,2,1,0:T(8,128)(2,1)} %get-tuple-element.80.refs_0_.refs_3_, bf16[2,3,128,768]{3,2,1,0:T(8,128)(2,1)} %copy-done.4, ...), custom_call_target="tpu_custom_call" | custom-call | tf_op jit(solution)/shard_map/regroup/pallas_call | solution.py:62
  73.1 3.1 %collective-permute-start.4 = (bf16[3,128,768]{2,1,0:T(8,128)(2,1)}, bf16[3,128,768]{2,1,0:T(8,128)(2,1)S(1)}, u32[]{:S(2)}, u32[]{:S(2)}) collective-permute-start(bf16[3,128,768]{2,1,0:T(8,128)(2,1)} %get-tuple-element.73), channel_id=1, source_target_pairs={{0,2},{1,3},{2,0},{3,1},{4,6},{5,7},{6,4},{7,5},{8,10},{9,11},{10,... | collective-permute-start | bytes 1769480 | tf_op jit(solution)/shard_map/ppermute | solution.py:408
  78.1 12.5 %collective-permute-done.4.refs_1_.refs_8_ = bf16[3,128,768]{2,1,0:T(8,128)(2,1)S(1)} collective-permute-done((bf16[3,128,768]{2,1,0:T(8,128)(2,1)}, bf16[3,128,768]{2,1,0:T(8,128)(2,1)S(1)}, u32[]{:S(2)}, u32[]{:S(2)}) %collective-permute-start.4) | collective-permute-done | bytes 589856 | tf_op jit(solution)/shard_map/ppermute | solution.py:408
  90.6 11.8 %collective-permute-done.5.refs_2_.refs_9_ = bf16[3,128,768]{2,1,0:T(8,128)(2,1)S(1)} collective-permute-done((bf16[3,128,768]{2,1,0:T(8,128)(2,1)}, bf16[3,128,768]{2,1,0:T(8,128)(2,1)S(1)}, u32[]{:S(2)}, u32[]{:S(2)}) %collective-permute-start.5) | collective-permute-done | bytes 589856 | tf_op jit(solution)/shard_map/ppermute | solution.py:408
  102.4 2.2 collective-permute-done.6.refs_3_.refs_10_
  104.6 2.9 %gather.2 = bf16[4,2,128,768]{3,2,1,0:T(8,128)(2,1)} custom-call(s32[3]{0:T(128)} %pad_add_fusion.position.refs_2_, bf16[4,3,128,768]{3,2,1,0:T(8,128)(2,1)} %copy-done.1, bf16[3,128,768]{2,1,0:T(8,128)(2,1)} %copy-done.5, bf16[3,128,768]{2,1,0:T(8,128)(2,1)} %copy-done.6, bf16[3,128,768]{2,1,0:T(8,128)(2,1)} %collective-permute-done.6.refs_3_.refs_10_), custom_call_target="tpu_custom_call" | custom-call | tf_op jit(solution)/shard_map/gather/pallas_call | solution.py:62
  107.6 3.0 %collective-permute-start.8 = (bf16[3,128,768]{2,1,0:T(8,128)(2,1)}, bf16[3,128,768]{2,1,0:T(8,128)(2,1)S(1)}, u32[]{:S(2)}, u32[]{:S(2)}) collective-permute-start(bf16[3,128,768]{2,1,0:T(8,128)(2,1)} %get-tuple-element.86), channel_id=1, source_target_pairs={{0,2},{1,3},{2,0},{3,1},{4,6},{5,7},{6,4},{7,5},{8,10},{9,11},{10,... | collective-permute-start | bytes 1769480 | tf_op jit(solution)/shard_map/ppermute | solution.py:408
  112.7 22.0 %attend.3 = bf16[8,128,768]{2,1,0:T(8,128)(2,1)} custom-call(s32[8]{0:T(128)} %bitcast.26, s32[16,16]{1,0:T(8,128)} %bitcast.23, s32[3]{0:T(128)} %pad_add_fusion.position.refs_2_, bf16[2,3,128,768]{3,2,1,0:T(8,128)(2,1)} %get-tuple-element.80.refs_0_.refs_3_, bf16[2,3,128,768]{3,2,1,0:T(8,128)(2,1)} %copy-done.4, ...), custom_call_target="tpu_custom_call" | custom-call | flops 3221225472 | bytes 9437184 | tf_op jit(solution)/shard_map/attend/pallas_call | solution.py:369
  134.7 4.2 %collective-permute-done.9.refs_2_.refs_5_ = bf16[3,128,768]{2,1,0:T(8,128)(2,1)S(1)} collective-permute-done((bf16[3,128,768]{2,1,0:T(8,128)(2,1)}, bf16[3,128,768]{2,1,0:T(8,128)(2,1)S(1)}, u32[]{:S(2)}, u32[]{:S(2)}) %collective-permute-start.9) | collective-permute-done | bytes 589856 | tf_op jit(solution)/shard_map/ppermute | solution.py:408
  140.4 2.9 %gather.3 = bf16[4,2,128,768]{3,2,1,0:T(8,128)(2,1)} custom-call(s32[3]{0:T(128)} %pad_add_fusion.position.refs_2_, bf16[3,128,768]{2,1,0:T(8,128)(2,1)} %get-tuple-element.94.refs_0_.refs_3_, bf16[3,128,768]{2,1,0:T(8,128)(2,1)} %copy-done.2, bf16[3,128,768]{2,1,0:T(8,128)(2,1)} %copy-done.3, bf16[3,128,768]{2,1,0:T(8,128)(2,1)} %collective-permute-done.10.refs_3_.refs_6_), custom_call_target="tpu_custom_call" | custom-call | tf_op jit(solution)/shard_map/gather/pallas_call | solution.py:62
  143.9 7.8 %all-to-all-start = ((bf16[8,128,768]{2,1,0:T(8,128)(2,1)}), bf16[8,128,768]{2,1,0:T(8,128)(2,1)}, u32[]{:S(2)}, u32[]{:S(2)}) async-start(bf16[8,128,768]{2,1,0:T(8,128)(2,1)} %attend.3), calls=%async_computation | async-start | bytes 3145728 | tf_op jit(solution)/shard_map/all_to_all | solution.py:427
  151.7 11.9 %attend.4 = (bf16[128,768]{1,0:T(8,128)(2,1)}, bf16[128,768]{1,0:T(8,128)(2,1)}, bf16[128,768]{1,0:T(8,128)(2,1)}, bf16[128,768]{1,0:T(8,128)(2,1)}) custom-call(s32[8]{0:T(128)} %bitcast.24, s32[16,16]{1,0:T(8,128)} %bitcast.21, s32[3]{0:T(128)} %pad_add_fusion.position.refs_2_, bf16[3,128,768]{2,1,0:T(8,128)(2,1)} %get-tuple-element.94.refs_0_.refs_3_, ...), custom_call_target="tpu_custom_call" | custom-call | flops 1610612736 | bytes 9437184 | tf_op jit(solution)/shard_map/attend/pallas_call | solution.py:369
  163.5 8.2 %collective-permute-start.16 = (bf16[128,768]{1,0:T(8,128)(2,1)}, bf16[128,768]{1,0:T(8,128)(2,1)S(1)}, u32[]{:S(2)}, u32[]{:S(2)}) collective-permute-start(bf16[128,768]{1,0:T(8,128)(2,1)} %get-tuple-element.105), channel_id=1, source_target_pairs={{0,250},{1,251},{2,248},{3,249},{4,254},{5,255},{6,252},{7,253},{8... | collective-permute-start | bytes 589832 | tf_op jit(solution)/shard_map/ppermute | solution.py:408
  171.8 2.8 %collective-permute-start.17 = (bf16[128,768]{1,0:T(8,128)(2,1)}, bf16[128,768]{1,0:T(8,128)(2,1)S(1)}, u32[]{:S(2)}, u32[]{:S(2)}) collective-permute-start(bf16[128,768]{1,0:T(8,128)(2,1)} %get-tuple-element.106), channel_id=1, source_target_pairs={{0,252},{1,253},{2,254},{3,255},{4,248},{5,249},{6,250},{7,251},{8... | collective-permute-start | bytes 589832 | tf_op jit(solution)/shard_map/ppermute | solution.py:408
  174.6 4.7 %collective-permute-start.18 = (bf16[128,768]{1,0:T(8,128)(2,1)}, bf16[128,768]{1,0:T(8,128)(2,1)S(1)}, u32[]{:S(2)}, u32[]{:S(2)}) collective-permute-start(bf16[128,768]{1,0:T(8,128)(2,1)} %get-tuple-element.107), channel_id=1, source_target_pairs={{0,254},{1,255},{2,252},{3,253},{4,250},{5,251},{6,248},{7,249},{8... | collective-permute-start | bytes 589832 | tf_op jit(solution)/shard_map/ppermute | solution.py:408
  179.3 13.2 %attend.5 = (bf16[128,768]{1,0:T(8,128)(2,1)}, bf16[128,768]{1,0:T(8,128)(2,1)}, bf16[128,768]{1,0:T(8,128)(2,1)}, bf16[128,768]{1,0:T(8,128)(2,1)}) custom-call(s32[8]{0:T(128)} %bitcast.25, s32[16,16]{1,0:T(8,128)} %bitcast.22, s32[3]{0:T(128)} %pad_add_fusion.position.refs_2_, bf16[3,128,768]{2,1,0:T(8,128)(2,1)} %get-tuple-element.94.refs_0_.refs_3_, ...), custom_call_target="tpu_custom_call" | custom-call | flops 1610612736 | bytes 9437184 | tf_op jit(solution)/shard_map/attend/pallas_call | solution.py:369
  192.6 2.8 %collective-permute-start.19 = (bf16[8,128,768]{2,1,0:T(8,128)(2,1)}, bf16[8,128,768]{2,1,0:T(8,128)(2,1)S(1)}, u32[]{:S(2)}, u32[]{:S(2)}) collective-permute-start(bf16[8,128,768]{2,1,0:T(8,128)(2,1)} %all-to-all-done), channel_id=1, source_target_pairs={{0,16},{1,17},{2,18},{3,19},{4,20},{5,21},{6,22},{7,23},{8,24},{9,... | collective-permute-start | bytes 4718600 | tf_op jit(solution)/shard_map/ppermute | solution.py:408
  196.8 2.5 %collective-permute-start.21 = (bf16[128,768]{1,0:T(8,128)(2,1)}, bf16[128,768]{1,0:T(8,128)(2,1)S(1)}, u32[]{:S(2)}, u32[]{:S(2)}) collective-permute-start(bf16[128,768]{1,0:T(8,128)(2,1)} %get-tuple-element.111), channel_id=1, source_target_pairs={{0,242},{1,243},{2,240},{3,241},{4,246},{5,247},{6,244},{7,245},{8... | collective-permute-start | bytes 589832 | tf_op jit(solution)/shard_map/ppermute | solution.py:408
  200.6 1.9 collective-permute-start.23
  202.6 5.9 %collective-permute-done.21.refs_1_ = bf16[128,768]{1,0:T(8,128)(2,1)S(1)} collective-permute-done((bf16[128,768]{1,0:T(8,128)(2,1)}, bf16[128,768]{1,0:T(8,128)(2,1)S(1)}, u32[]{:S(2)}, u32[]{:S(2)}) %collective-permute-start.21) | collective-permute-done | bytes 196640 | tf_op jit(solution)/shard_map/ppermute | solution.py:408
  208.5 5.4 %collective-permute-done.22.refs_2_ = bf16[128,768]{1,0:T(8,128)(2,1)S(1)} collective-permute-done((bf16[128,768]{1,0:T(8,128)(2,1)}, bf16[128,768]{1,0:T(8,128)(2,1)S(1)}, u32[]{:S(2)}, u32[]{:S(2)}) %collective-permute-start.22) | collective-permute-done | bytes 196640 | tf_op jit(solution)/shard_map/ppermute | solution.py:408
  215.8 3.0 %join.3 = bf16[128,6144]{1,0:T(8,128)(2,1)} custom-call(s32[3]{0:T(128)} %pad_add_fusion.position.refs_2_, bf16[128,768]{1,0:T(8,128)(2,1)} %copy-done.12, bf16[128,768]{1,0:T(8,128)(2,1)} %copy-done.13, bf16[128,768]{1,0:T(8,128)(2,1)} %copy-done.14, bf16[128,768]{1,0:T(8,128)(2,1)} %copy-done.15, bf16[128,768]{1,0:T(8,128)(2,1)} %copy-done.11, ...), custom_call_target="tpu_custom_call" | custom-call | tf_op jit(solution)/shard_map/join/pallas_call | solution.py:62
  218.8 11.9 %collective-permute-done.19.refs_0_ = bf16[8,128,768]{2,1,0:T(8,128)(2,1)S(1)} collective-permute-done((bf16[8,128,768]{2,1,0:T(8,128)(2,1)}, bf16[8,128,768]{2,1,0:T(8,128)(2,1)S(1)}, u32[]{:S(2)}, u32[]{:S(2)}) %collective-permute-start.19) | collective-permute-done | bytes 1572896 | tf_op jit(solution)/shard_map/ppermute | solution.py:408
  231.8 3.0 %join.2 = bf16[128,6144]{1,0:T(8,128)(2,1)} custom-call(s32[3]{0:T(128)} %pad_add_fusion.position.refs_2_, bf16[8,128,768]{2,1,0:T(8,128)(2,1)} %copy-done.7), custom_call_target="tpu_custom_call" | custom-call | tf_op jit(solution)/shard_map/join/pallas_call | solution.py:62
  (63 shorter events, 16.9 us)
Async XLA Ops:
  4.6 54.8 %collective-permute-start.3 = (bf16[4,3,128,768]{3,2,1,0:T(8,128)(2,1)}, bf16[4,3,128,768]{3,2,1,0:T(8,128)(2,1)S(1)}, u32[]{:S(2)}, u32[]{:S(2)}) collective-permute-start(bf16[4,3,128,768]{3,2,1,0:T(8,128)(2,1)} %cut_side.1), channel_id=1, source_target_pairs={{0,8},{1,9},{2,10},{3,11},{4,12},{5,13},{6,14},{7,15},{8,0},{9,1},... | collective-permute-start | bytes 7077896 | tf_op jit(solution)/shard_map/ppermute | solution.py:408
  12.7 51.1 %collective-permute-start = (bf16[2,3,128,768]{3,2,1,0:T(8,128)(2,1)}, bf16[2,3,128,768]{3,2,1,0:T(8,128)(2,1)S(1)}, u32[]{:S(2)}, u32[]{:S(2)}) collective-permute-start(bf16[2,3,128,768]{3,2,1,0:T(8,128)(2,1)} %get-tuple-element.62), channel_id=1, source_target_pairs={{0,2},{1,3},{2,0},{3,1},{4,6},{5,7},{6,4},{7,5},{8,10},{9,11},{10,... | collective-permute-start | bytes 3538952 | tf_op jit(solution)/shard_map/ppermute | solution.py:408
  13.4 53.5 %collective-permute-start.1 = (bf16[2,3,128,768]{3,2,1,0:T(8,128)(2,1)}, bf16[2,3,128,768]{3,2,1,0:T(8,128)(2,1)}, u32[]{:S(2)}, u32[]{:S(2)}) collective-permute-start(bf16[2,3,128,768]{3,2,1,0:T(8,128)(2,1)} %get-tuple-element.63), channel_id=1, source_target_pairs={{0,4},{1,5},{2,6},{3,7},{4,0},{5,1},{6,2},{7,3},{8,12},{9,13},{10,... | collective-permute-start | bytes 3538952 | tf_op jit(solution)/shard_map/ppermute | solution.py:408
  15.8 52.5 %collective-permute-start.2 = (bf16[2,3,128,768]{3,2,1,0:T(8,128)(2,1)}, bf16[2,3,128,768]{3,2,1,0:T(8,128)(2,1)}, u32[]{:S(2)}, u32[]{:S(2)}) collective-permute-start(bf16[2,3,128,768]{3,2,1,0:T(8,128)(2,1)} %get-tuple-element.64), channel_id=1, source_target_pairs={{0,6},{1,7},{2,4},{3,5},{4,2},{5,3},{6,0},{7,1},{8,14},{9,15},{10,... | collective-permute-start | bytes 3538952 | tf_op jit(solution)/shard_map/ppermute | solution.py:408
  73.0 31.5 %collective-permute-start.7 = (bf16[4,3,128,768]{3,2,1,0:T(8,128)(2,1)}, bf16[4,3,128,768]{3,2,1,0:T(8,128)(2,1)}, u32[]{:S(2)}, u32[]{:S(2)}) collective-permute-start(bf16[4,3,128,768]{3,2,1,0:T(8,128)(2,1)} %get-tuple-element.84), channel_id=1, source_target_pairs={{0,1},{1,0},{2,3},{3,2},{4,5},{5,4},{6,7},{7,6},{8,9},{9,8},{10,11... | collective-permute-start | bytes 7077896 | tf_op jit(solution)/shard_map/ppermute | solution.py:408
  73.1 17.5 %collective-permute-start.4 = (bf16[3,128,768]{2,1,0:T(8,128)(2,1)}, bf16[3,128,768]{2,1,0:T(8,128)(2,1)S(1)}, u32[]{:S(2)}, u32[]{:S(2)}) collective-permute-start(bf16[3,128,768]{2,1,0:T(8,128)(2,1)} %get-tuple-element.73), channel_id=1, source_target_pairs={{0,2},{1,3},{2,0},{3,1},{4,6},{5,7},{6,4},{7,5},{8,10},{9,11},{10,... | collective-permute-start | bytes 1769480 | tf_op jit(solution)/shard_map/ppermute | solution.py:408
  76.2 26.2 %collective-permute-start.5 = (bf16[3,128,768]{2,1,0:T(8,128)(2,1)}, bf16[3,128,768]{2,1,0:T(8,128)(2,1)S(1)}, u32[]{:S(2)}, u32[]{:S(2)}) collective-permute-start(bf16[3,128,768]{2,1,0:T(8,128)(2,1)} %get-tuple-element.74), channel_id=1, source_target_pairs={{0,4},{1,5},{2,6},{3,7},{4,0},{5,1},{6,2},{7,3},{8,12},{9,13},{10,... | collective-permute-start | bytes 1769480 | tf_op jit(solution)/shard_map/ppermute | solution.py:408
  76.2 28.3 %collective-permute-start.6 = (bf16[3,128,768]{2,1,0:T(8,128)(2,1)}, bf16[3,128,768]{2,1,0:T(8,128)(2,1)}, u32[]{:S(2)}, u32[]{:S(2)}) collective-permute-start(bf16[3,128,768]{2,1,0:T(8,128)(2,1)} %get-tuple-element.75), channel_id=1, source_target_pairs={{0,6},{1,7},{2,4},{3,5},{4,2},{5,3},{6,0},{7,1},{8,14},{9,15},{10,... | collective-permute-start | bytes 1769480 | tf_op jit(solution)/shard_map/ppermute | solution.py:408
  77.8 56.9 %collective-permute-start.11 = (bf16[4,3,128,768]{3,2,1,0:T(8,128)(2,1)}, bf16[4,3,128,768]{3,2,1,0:T(8,128)(2,1)S(1)}, u32[]{:S(2)}, u32[]{:S(2)}) collective-permute-start(bf16[4,3,128,768]{3,2,1,0:T(8,128)(2,1)} %get-tuple-element.89), channel_id=1, source_target_pairs={{0,8},{1,9},{2,10},{3,11},{4,12},{5,13},{6,14},{7,15},{8,0},{9,1},... | collective-permute-start | bytes 7077896 | tf_op jit(solution)/shard_map/ppermute | solution.py:408
  90.6 14.0 %copy-start.5 = (bf16[3,128,768]{2,1,0:T(8,128)(2,1)}, bf16[3,128,768]{2,1,0:T(8,128)(2,1)S(1)}, u32[]{:S(2)}) copy-start(bf16[3,128,768]{2,1,0:T(8,128)(2,1)S(1)} %collective-permute-done.4.refs_1_.refs_8_) | copy-start | bytes 1769476
  107.5 5.2 %collective-permute-start.12 = (bf16[4,2,128,768]{3,2,1,0:T(8,128)(2,1)}, bf16[4,2,128,768]{3,2,1,0:T(8,128)(2,1)}, u32[]{:S(2)}, u32[]{:S(2)}) collective-permute-start(bf16[4,2,128,768]{3,2,1,0:T(8,128)(2,1)} %gather.2), channel_id=1, source_target_pairs={{0,1},{1,0},{2,3},{3,2},{4,5},{5,4},{6,7},{7,6},{8,9},{9,8},{10,11... | collective-permute-start | bytes 4718600 | tf_op jit(solution)/shard_map/ppermute | solution.py:408
  107.6 27.2 %collective-permute-start.8 = (bf16[3,128,768]{2,1,0:T(8,128)(2,1)}, bf16[3,128,768]{2,1,0:T(8,128)(2,1)S(1)}, u32[]{:S(2)}, u32[]{:S(2)}) collective-permute-start(bf16[3,128,768]{2,1,0:T(8,128)(2,1)} %get-tuple-element.86), channel_id=1, source_target_pairs={{0,2},{1,3},{2,0},{3,1},{4,6},{5,7},{6,4},{7,5},{8,10},{9,11},{10,... | collective-permute-start | bytes 1769480 | tf_op jit(solution)/shard_map/ppermute | solution.py:408
  110.5 28.4 %collective-permute-start.9 = (bf16[3,128,768]{2,1,0:T(8,128)(2,1)}, bf16[3,128,768]{2,1,0:T(8,128)(2,1)S(1)}, u32[]{:S(2)}, u32[]{:S(2)}) collective-permute-start(bf16[3,128,768]{2,1,0:T(8,128)(2,1)} %get-tuple-element.87), channel_id=1, source_target_pairs={{0,4},{1,5},{2,6},{3,7},{4,0},{5,1},{6,2},{7,3},{8,12},{9,13},{10,... | collective-permute-start | bytes 1769480 | tf_op jit(solution)/shard_map/ppermute | solution.py:408
  112.2 28.2 %collective-permute-start.10 = (bf16[3,128,768]{2,1,0:T(8,128)(2,1)}, bf16[3,128,768]{2,1,0:T(8,128)(2,1)}, u32[]{:S(2)}, u32[]{:S(2)}) collective-permute-start(bf16[3,128,768]{2,1,0:T(8,128)(2,1)} %get-tuple-element.88), channel_id=1, source_target_pairs={{0,6},{1,7},{2,4},{3,5},{4,2},{5,3},{6,0},{7,1},{8,14},{9,15},{10,... | collective-permute-start | bytes 1769480 | tf_op jit(solution)/shard_map/ppermute | solution.py:408
  134.7 8.6 %copy-start = (bf16[4,3,128,768]{3,2,1,0:T(8,128)(2,1)}, bf16[4,3,128,768]{3,2,1,0:T(8,128)(2,1)S(1)}, u32[]{:S(2)}) copy-start(bf16[4,3,128,768]{3,2,1,0:T(8,128)(2,1)S(1)} %collective-permute-done.11.refs_7_.refs_8_.refs_9_.refs_10_) | copy-start | bytes 7077892
  140.4 11.2 %collective-permute-start.14 = (bf16[4,3,128,768]{3,2,1,0:T(8,128)(2,1)S(1)}, bf16[4,3,128,768]{3,2,1,0:T(8,128)(2,1)}, u32[]{:S(2)}, u32[]{:S(2)}) collective-permute-start(bf16[4,3,128,768]{3,2,1,0:T(8,128)(2,1)S(1)} %collective-permute-done.11.refs_7_.refs_8_.refs_9_.refs_10_), channel_id=1, source_target_pairs={{0,1},{1,0},{2,3},{3,2},{4,5},{5,4},{6,7},{7,6},{8,9},{9,8},{10,11... | collective-permute-start | bytes 7077896 | tf_op jit(solution)/shard_map/ppermute | solution.py:408
  143.3 8.4 %collective-permute-start.13 = (bf16[4,2,128,768]{3,2,1,0:T(8,128)(2,1)}, bf16[4,2,128,768]{3,2,1,0:T(8,128)(2,1)}, u32[]{:S(2)}, u32[]{:S(2)}) collective-permute-start(bf16[4,2,128,768]{3,2,1,0:T(8,128)(2,1)} %gather.3), channel_id=1, source_target_pairs={{0,1},{1,0},{2,3},{3,2},{4,5},{5,4},{6,7},{7,6},{8,9},{9,8},{10,11... | collective-permute-start | bytes 4718600 | tf_op jit(solution)/shard_map/ppermute | solution.py:408
  143.9 48.6 %all-to-all-start = ((bf16[8,128,768]{2,1,0:T(8,128)(2,1)}), bf16[8,128,768]{2,1,0:T(8,128)(2,1)}, u32[]{:S(2)}, u32[]{:S(2)}) async-start(bf16[8,128,768]{2,1,0:T(8,128)(2,1)} %attend.3), calls=%async_computation | async-start | bytes 3145728 | tf_op jit(solution)/shard_map/all_to_all | solution.py:427
  163.5 29.0 %collective-permute-start.16 = (bf16[128,768]{1,0:T(8,128)(2,1)}, bf16[128,768]{1,0:T(8,128)(2,1)S(1)}, u32[]{:S(2)}, u32[]{:S(2)}) collective-permute-start(bf16[128,768]{1,0:T(8,128)(2,1)} %get-tuple-element.105), channel_id=1, source_target_pairs={{0,250},{1,251},{2,248},{3,249},{4,254},{5,255},{6,252},{7,253},{8... | collective-permute-start | bytes 589832 | tf_op jit(solution)/shard_map/ppermute | solution.py:408
  171.8 20.8 %collective-permute-start.17 = (bf16[128,768]{1,0:T(8,128)(2,1)}, bf16[128,768]{1,0:T(8,128)(2,1)S(1)}, u32[]{:S(2)}, u32[]{:S(2)}) collective-permute-start(bf16[128,768]{1,0:T(8,128)(2,1)} %get-tuple-element.106), channel_id=1, source_target_pairs={{0,252},{1,253},{2,254},{3,255},{4,248},{5,249},{6,250},{7,251},{8... | collective-permute-start | bytes 589832 | tf_op jit(solution)/shard_map/ppermute | solution.py:408
  174.6 18.0 %collective-permute-start.18 = (bf16[128,768]{1,0:T(8,128)(2,1)}, bf16[128,768]{1,0:T(8,128)(2,1)S(1)}, u32[]{:S(2)}, u32[]{:S(2)}) collective-permute-start(bf16[128,768]{1,0:T(8,128)(2,1)} %get-tuple-element.107), channel_id=1, source_target_pairs={{0,254},{1,255},{2,252},{3,253},{4,250},{5,251},{6,248},{7,249},{8... | collective-permute-start | bytes 589832 | tf_op jit(solution)/shard_map/ppermute | solution.py:408
  179.3 13.3 %collective-permute-start.15 = (bf16[128,768]{1,0:T(8,128)(2,1)}, bf16[128,768]{1,0:T(8,128)(2,1)S(1)}, u32[]{:S(2)}, u32[]{:S(2)}) collective-permute-start(bf16[128,768]{1,0:T(8,128)(2,1)} %get-tuple-element.99), channel_id=1, source_target_pairs={{0,248},{1,249},{2,250},{3,251},{4,252},{5,253},{6,254},{7,255},{8... | collective-permute-start | bytes 589832 | tf_op jit(solution)/shard_map/ppermute | solution.py:408
  192.5 22.6 %copy-start.8 = (bf16[128,768]{1,0:T(8,128)(2,1)}, bf16[128,768]{1,0:T(8,128)(2,1)S(1)}, u32[]{:S(2)}) copy-start(bf16[128,768]{1,0:T(8,128)(2,1)S(1)} %collective-permute-done.16.refs_5_) | copy-start | bytes 589828
  192.6 22.5 %copy-start.9 = (bf16[128,768]{1,0:T(8,128)(2,1)}, bf16[128,768]{1,0:T(8,128)(2,1)S(1)}, u32[]{:S(2)}) copy-start(bf16[128,768]{1,0:T(8,128)(2,1)S(1)} %collective-permute-done.17.refs_6_) | copy-start | bytes 589828
  192.6 22.5 %copy-start.10 = (bf16[128,768]{1,0:T(8,128)(2,1)}, bf16[128,768]{1,0:T(8,128)(2,1)S(1)}, u32[]{:S(2)}) copy-start(bf16[128,768]{1,0:T(8,128)(2,1)S(1)} %collective-permute-done.18.refs_7_) | copy-start | bytes 589828
  192.6 22.5 %copy-start.11 = (bf16[128,768]{1,0:T(8,128)(2,1)}, bf16[128,768]{1,0:T(8,128)(2,1)S(1)}, u32[]{:S(2)}) copy-start(bf16[128,768]{1,0:T(8,128)(2,1)S(1)} %collective-permute-done.15.refs_4_) | copy-start | bytes 589828
  192.6 38.0 %collective-permute-start.19 = (bf16[8,128,768]{2,1,0:T(8,128)(2,1)}, bf16[8,128,768]{2,1,0:T(8,128)(2,1)S(1)}, u32[]{:S(2)}, u32[]{:S(2)}) collective-permute-start(bf16[8,128,768]{2,1,0:T(8,128)(2,1)} %all-to-all-done), channel_id=1, source_target_pairs={{0,16},{1,17},{2,18},{3,19},{4,20},{5,21},{6,22},{7,23},{8,24},{9,... | collective-permute-start | bytes 4718600 | tf_op jit(solution)/shard_map/ppermute | solution.py:408
  195.4 7.2 %collective-permute-start.20 = (bf16[128,768]{1,0:T(8,128)(2,1)}, bf16[128,768]{1,0:T(8,128)(2,1)S(1)}, u32[]{:S(2)}, u32[]{:S(2)}) collective-permute-start(bf16[128,768]{1,0:T(8,128)(2,1)} %get-tuple-element.110), channel_id=1, source_target_pairs={{0,240},{1,241},{2,242},{3,243},{4,244},{5,245},{6,246},{7,247},{8... | collective-permute-start | bytes 589832 | tf_op jit(solution)/shard_map/ppermute | solution.py:408
  196.8 11.7 %collective-permute-start.21 = (bf16[128,768]{1,0:T(8,128)(2,1)}, bf16[128,768]{1,0:T(8,128)(2,1)S(1)}, u32[]{:S(2)}, u32[]{:S(2)}) collective-permute-start(bf16[128,768]{1,0:T(8,128)(2,1)} %get-tuple-element.111), channel_id=1, source_target_pairs={{0,242},{1,243},{2,240},{3,241},{4,246},{5,247},{6,244},{7,245},{8... | collective-permute-start | bytes 589832 | tf_op jit(solution)/shard_map/ppermute | solution.py:408
  199.3 14.5 %collective-permute-start.22 = (bf16[128,768]{1,0:T(8,128)(2,1)}, bf16[128,768]{1,0:T(8,128)(2,1)S(1)}, u32[]{:S(2)}, u32[]{:S(2)}) collective-permute-start(bf16[128,768]{1,0:T(8,128)(2,1)} %get-tuple-element.112), channel_id=1, source_target_pairs={{0,244},{1,245},{2,246},{3,247},{4,240},{5,241},{6,242},{7,243},{8... | collective-permute-start | bytes 589832 | tf_op jit(solution)/shard_map/ppermute | solution.py:408
  200.6 14.5 %collective-permute-start.23 = (bf16[128,768]{1,0:T(8,128)(2,1)}, bf16[128,768]{1,0:T(8,128)(2,1)S(1)}, u32[]{:S(2)}, u32[]{:S(2)}) collective-permute-start(bf16[128,768]{1,0:T(8,128)(2,1)} %get-tuple-element.113), channel_id=1, source_target_pairs={{0,246},{1,247},{2,244},{3,245},{4,242},{5,243},{6,240},{7,241},{8... | collective-permute-start | bytes 589832 | tf_op jit(solution)/shard_map/ppermute | solution.py:408
  202.6 12.5 %copy-start.12 = (bf16[128,768]{1,0:T(8,128)(2,1)}, bf16[128,768]{1,0:T(8,128)(2,1)S(1)}, u32[]{:S(2)}) copy-start(bf16[128,768]{1,0:T(8,128)(2,1)S(1)} %collective-permute-done.20.refs_0_) | copy-start | bytes 589828
  (9 other events, 25.0 us)

commit v3 on v2

--- a/solution.py
+++ b/solution.py
@@ -199,26 +199,27 @@
             (position[1] ^ (piece % CHIPS)) * 2 + core
         )
 
-    copies = []
+    early, late = [], []
     for piece in range(2 * CHIPS):
         if apart:
             slot = piece % CHIPS
         else:
             slot = block_of(piece, core) // 2
+        mine = part(pieces[piece], places[piece])
         if side in (None, piece // CHIPS):
-            copies.append((part(pieces[piece], places[piece]).at[0], asked.at[slot]))
-        mine = part(pieces[piece], places[piece]).at[pl.ds(1, 2)]
-        copies.append((mine, held.at[block_of(piece, core)]))
+            early.append((mine.at[0], asked.at[slot]))
         other = (near_other if piece < CHIPS else far_other).at[piece % CHIPS]
-        if other.shape[0] == 3:
-            other = other.at[pl.ds(1, 2)]
-        copies.append((other, held.at[block_of(piece, 1 - core)]))
+        extra = other.shape[0] - 2
+        for kind, copies in ((0, early), (1, late)):
+            copies.append((mine.at[1 + kind], held.at[block_of(piece, core), kind]))
+            copies.append((other.at[extra + kind], held.at[block_of(piece, 1 - core), kind]))
     copies = [
         pltpu.make_async_copy(source, target, arrived.at[index])
-        for index, (source, target) in enumerate(copies)
+        for index, (source, target) in enumerate(early + late)
     ]
     for copy in copies:
         copy.start()
+    early, late = copies[: len(early)], copies[len(early) :]
 
     bounds = []
     bound = jnp.int32(0)
@@ -232,7 +233,7 @@
             found = found + (tokens >= bound).astype(jnp.int32)
         return found
 
-    for copy in copies:
+    for copy in early:
         copy.wait()
 
     def rows(step, _):
@@ -313,6 +314,11 @@
                     jnp.max(largest[head], axis=1, keepdims=True), (tile, BLOCK)
                 )
 
+            @pl.when((step == 0) & (group == 0))
+            def _():
+                for copy in late:
+                    copy.wait()
+
             def combine(chunk, _):
                 columns = [jnp.maximum(listed[chunk * WIDE + part], 0) for part in range(WIDE)]
                 for head in range(group_heads):
@@ -382,7 +388,7 @@
             per_head,
             per_head,
             pltpu.SMEM((blocks + WIDE,), jnp.int32),
-            pltpu.SemaphoreType.DMA((6 * CHIPS,)),
+            pltpu.SemaphoreType.DMA((10 * CHIPS,)),
         ],
         compiler_params=pltpu.CompilerParams(vmem_limit_bytes=CUT_VMEM),
         cost_estimate=pl.CostEstimate(

time: 238 us -> 237 us (level)
  Pallas kernels: 77.8 us -> 70.6 us
  starting transfers between devices: 51.1 us -> 55.1 us
  waiting for transfers between devices: 101 us -> 104 us
    pallas_call x3, Pallas kernels: 47.1 us -> 39.9 us  [attend(): pl.pallas_call(kernel, out_shape=[jax.ShapeDtypeStruct((BLOCK, width), jn...]
    ppermute x24, starting transfers between devices: 43.4 us -> 47.3 us  [moved(): return lax.ppermute(value, ('section', 'ctx'), pairs)]
    ppermute x24, waiting for transfers between devices: 101 us -> 104 us  [moved(): return lax.ppermute(value, ('section', 'ctx'), pairs)]
  transfers between devices with their start and end apart: 25 -> 25, of which waited for: 13 -> 13; matrix products, arithmetic and copies ran while one was open for 0% -> 0% of each run, Pallas kernels for 28% -> 25%
where the time goes in v3:
time: 237 us; the launch traced here: 235 us
  waiting for transfers between devices  104 us (44%)
  Pallas kernels  70.6 us (30%)
  starting transfers between devices  55.1 us (23%)
  local copies, waits for them, and re-layouts  3.34 us (1%)
    ppermute x24, waiting for transfers between devices, moved(): return lax.ppermute(value, ('section', 'ctx'), pairs)  104 us
    ppermute x24, starting transfers between devices, moved(): return lax.ppermute(value, ('section', 'ctx'), pairs)  47.3 us
    pallas_call x3, Pallas kernels, attend(): pl.pallas_call(kernel, out_shape=[jax.ShapeDtypeStruct((BLOCK, width), jn...  39.9 us
    pallas_call x9, Pallas kernels, copied(): pl.pallas_call(kernel, out_shape=[jax.ShapeDtypeStruct(shape, jnp.bfloat1...  30.7 us
    all_to_all x1, starting transfers between devices, spread(): lax.all_to_all(pieces, 'ctx', split_axis=0, concat_axis=0, axis_index_gro...  7.76 us
  transfers between devices with their start and end apart: 25, of which 13 were waited for; matrix products, arithmetic and copies ran while one was open for 0% of the time, Pallas kernels for 25%

profile of v3, /device:TPU:2, one launch (start us, length us, event | category | flops | bytes accessed | tf_op | source)
XLA Modules:
  0.0 234.6 jit_solution(2050463531287715125)
XLA Ops:
  1.3 3.2 %cut_side.1 = bf16[4,3,128,768]{3,2,1,0:T(8,128)(2,1)} custom-call(s32[3]{0:T(128)} %pad_add_fusion.position.refs_2_, bf16[3,128,6144]{2,1,0:T(8,128)(2,1)} %bitcast.15), custom_call_target="tpu_custom_call" | custom-call | tf_op jit(solution)/shard_map/cut_side/pallas_call | solution.py:62
  4.6 3.3 %collective-permute-start.3 = (bf16[4,3,128,768]{3,2,1,0:T(8,128)(2,1)}, bf16[4,3,128,768]{3,2,1,0:T(8,128)(2,1)S(1)}, u32[]{:S(2)}, u32[]{:S(2)}) collective-permute-start(bf16[4,3,128,768]{3,2,1,0:T(8,128)(2,1)} %cut_side.1), channel_id=1, source_target_pairs={{0,8},{1,9},{2,10},{3,11},{4,12},{5,13},{6,14},{7,15},{8,0},{9,1},... | collective-permute-start | bytes 7077896 | tf_op jit(solution)/shard_map/ppermute | solution.py:414
  7.8 4.9 %cut_both.1 = (bf16[2,3,128,768]{3,2,1,0:T(8,128)(2,1)}, bf16[2,3,128,768]{3,2,1,0:T(8,128)(2,1)}, bf16[2,3,128,768]{3,2,1,0:T(8,128)(2,1)}, bf16[2,3,128,768]{3,2,1,0:T(8,128)(2,1)}) custom-call(s32[3]{0:T(128)} %pad_add_fusion.position.refs_2_, bf16[3,128,6144]{2,1,0:T(8,128)(2,1)} %bitcast.16, bf16[3,128,6144]{2,1,0:T(8,128)(2,1)} %bitcast.17), custom_call_target="tpu_custom_call" | custom-call | tf_op jit(solution)/shard_map/cut_both/pallas_call | solution.py:62
  13.4 2.4 %collective-permute-start.1 = (bf16[2,3,128,768]{3,2,1,0:T(8,128)(2,1)}, bf16[2,3,128,768]{3,2,1,0:T(8,128)(2,1)}, u32[]{:S(2)}, u32[]{:S(2)}) collective-permute-start(bf16[2,3,128,768]{3,2,1,0:T(8,128)(2,1)} %get-tuple-element.63), channel_id=1, source_target_pairs={{0,4},{1,5},{2,6},{3,7},{4,0},{5,1},{6,2},{7,3},{8,12},{9,13},{10,... | collective-permute-start | bytes 3538952 | tf_op jit(solution)/shard_map/ppermute | solution.py:414
  16.3 3.2 %cut_each.1 = (bf16[3,128,768]{2,1,0:T(8,128)(2,1)}, bf16[3,128,768]{2,1,0:T(8,128)(2,1)}, bf16[3,128,768]{2,1,0:T(8,128)(2,1)}, bf16[3,128,768]{2,1,0:T(8,128)(2,1)}) custom-call(s32[3]{0:T(128)} %pad_add_fusion.position.refs_2_, bf16[3,128,6144]{2,1,0:T(8,128)(2,1)} %bitcast.18), custom_call_target="tpu_custom_call" | custom-call | tf_op jit(solution)/shard_map/cut_each/pallas_call | solution.py:62
  19.5 39.8 %collective-permute-done.3.refs_0_.refs_7_ = bf16[4,3,128,768]{3,2,1,0:T(8,128)(2,1)S(1)} collective-permute-done((bf16[4,3,128,768]{3,2,1,0:T(8,128)(2,1)}, bf16[4,3,128,768]{3,2,1,0:T(8,128)(2,1)S(1)}, u32[]{:S(2)}, u32[]{:S(2)}) %collective-permute-start.3) | collective-permute-done | bytes 2359328 | tf_op jit(solution)/shard_map/ppermute | solution.py:414
  60.8 3.0 %separate.1 = (bf16[3,128,768]{2,1,0:T(8,128)(2,1)}, bf16[3,128,768]{2,1,0:T(8,128)(2,1)}, bf16[3,128,768]{2,1,0:T(8,128)(2,1)}) custom-call(s32[3]{0:T(128)} %pad_add_fusion.position.refs_2_, bf16[4,3,128,768]{3,2,1,0:T(8,128)(2,1)} %copy-done.1), custom_call_target="tpu_custom_call" | custom-call | tf_op jit(solution)/shard_map/separate/pallas_call | solution.py:62
  63.8 3.1 %collective-permute-done.1.refs_2_.refs_5_ = bf16[2,3,128,768]{3,2,1,0:T(8,128)(2,1)} collective-permute-done((bf16[2,3,128,768]{3,2,1,0:T(8,128)(2,1)}, bf16[2,3,128,768]{3,2,1,0:T(8,128)(2,1)}, u32[]{:S(2)}, u32[]{:S(2)}) %collective-permute-start.1) | collective-permute-done | bytes 1179680 | tf_op jit(solution)/shard_map/ppermute | solution.py:414
  68.2 4.8 %regroup.1 = (bf16[4,3,128,768]{3,2,1,0:T(8,128)(2,1)}, bf16[4,3,128,768]{3,2,1,0:T(8,128)(2,1)}) custom-call(s32[3]{0:T(128)} %pad_add_fusion.position.refs_2_, bf16[2,3,128,768]{3,2,1,0:T(8,128)(2,1)} %get-tuple-element.80.refs_0_.refs_3_, bf16[2,3,128,768]{3,2,1,0:T(8,128)(2,1)} %copy-done.4, ...), custom_call_target="tpu_custom_call" | custom-call | tf_op jit(solution)/shard_map/regroup/pallas_call | solution.py:62
  73.1 3.1 %collective-permute-start.4 = (bf16[3,128,768]{2,1,0:T(8,128)(2,1)}, bf16[3,128,768]{2,1,0:T(8,128)(2,1)S(1)}, u32[]{:S(2)}, u32[]{:S(2)}) collective-permute-start(bf16[3,128,768]{2,1,0:T(8,128)(2,1)} %get-tuple-element.73), channel_id=1, source_target_pairs={{0,2},{1,3},{2,0},{3,1},{4,6},{5,7},{6,4},{7,5},{8,10},{9,11},{10,... | collective-permute-start | bytes 1769480 | tf_op jit(solution)/shard_map/ppermute | solution.py:414
  78.1 12.5 %collective-permute-done.4.refs_1_.refs_8_ = bf16[3,128,768]{2,1,0:T(8,128)(2,1)S(1)} collective-permute-done((bf16[3,128,768]{2,1,0:T(8,128)(2,1)}, bf16[3,128,768]{2,1,0:T(8,128)(2,1)S(1)}, u32[]{:S(2)}, u32[]{:S(2)}) %collective-permute-start.4) | collective-permute-done | bytes 589856 | tf_op jit(solution)/shard_map/ppermute | solution.py:414
  90.6 11.8 %collective-permute-done.5.refs_2_.refs_9_ = bf16[3,128,768]{2,1,0:T(8,128)(2,1)S(1)} collective-permute-done((bf16[3,128,768]{2,1,0:T(8,128)(2,1)}, bf16[3,128,768]{2,1,0:T(8,128)(2,1)S(1)}, u32[]{:S(2)}, u32[]{:S(2)}) %collective-permute-start.5) | collective-permute-done | bytes 589856 | tf_op jit(solution)/shard_map/ppermute | solution.py:414
  104.6 2.9 %gather.2 = bf16[4,2,128,768]{3,2,1,0:T(8,128)(2,1)} custom-call(s32[3]{0:T(128)} %pad_add_fusion.position.refs_2_, bf16[4,3,128,768]{3,2,1,0:T(8,128)(2,1)} %copy-done.1, bf16[3,128,768]{2,1,0:T(8,128)(2,1)} %copy-done.5, bf16[3,128,768]{2,1,0:T(8,128)(2,1)} %copy-done.6, bf16[3,128,768]{2,1,0:T(8,128)(2,1)} %collective-permute-done.6.refs_3_.refs_10_), custom_call_target="tpu_custom_call" | custom-call | tf_op jit(solution)/shard_map/gather/pallas_call | solution.py:62
  107.6 3.0 %collective-permute-start.8 = (bf16[3,128,768]{2,1,0:T(8,128)(2,1)}, bf16[3,128,768]{2,1,0:T(8,128)(2,1)S(1)}, u32[]{:S(2)}, u32[]{:S(2)}) collective-permute-start(bf16[3,128,768]{2,1,0:T(8,128)(2,1)} %get-tuple-element.86), channel_id=1, source_target_pairs={{0,2},{1,3},{2,0},{3,1},{4,6},{5,7},{6,4},{7,5},{8,10},{9,11},{10,... | collective-permute-start | bytes 1769480 | tf_op jit(solution)/shard_map/ppermute | solution.py:414
  112.7 18.8 %attend.3 = bf16[8,128,768]{2,1,0:T(8,128)(2,1)} custom-call(s32[8]{0:T(128)} %bitcast.26, s32[16,16]{1,0:T(8,128)} %bitcast.23, s32[3]{0:T(128)} %pad_add_fusion.position.refs_2_, bf16[2,3,128,768]{3,2,1,0:T(8,128)(2,1)} %get-tuple-element.80.refs_0_.refs_3_, bf16[2,3,128,768]{3,2,1,0:T(8,128)(2,1)} %copy-done.4, ...), custom_call_target="tpu_custom_call" | custom-call | flops 3221225472 | bytes 9437184 | tf_op jit(solution)/shard_map/attend/pallas_call | solution.py:375
  132.4 6.5 %collective-permute-done.9.refs_2_.refs_5_ = bf16[3,128,768]{2,1,0:T(8,128)(2,1)S(1)} collective-permute-done((bf16[3,128,768]{2,1,0:T(8,128)(2,1)}, bf16[3,128,768]{2,1,0:T(8,128)(2,1)S(1)}, u32[]{:S(2)}, u32[]{:S(2)}) %collective-permute-start.9) | collective-permute-done | bytes 589856 | tf_op jit(solution)/shard_map/ppermute | solution.py:414
  140.4 2.9 %gather.3 = bf16[4,2,128,768]{3,2,1,0:T(8,128)(2,1)} custom-call(s32[3]{0:T(128)} %pad_add_fusion.position.refs_2_, bf16[3,128,768]{2,1,0:T(8,128)(2,1)} %get-tuple-element.94.refs_0_.refs_3_, bf16[3,128,768]{2,1,0:T(8,128)(2,1)} %copy-done.2, bf16[3,128,768]{2,1,0:T(8,128)(2,1)} %copy-done.3, bf16[3,128,768]{2,1,0:T(8,128)(2,1)} %collective-permute-done.10.refs_3_.refs_6_), custom_call_target="tpu_custom_call" | custom-call | tf_op jit(solution)/shard_map/gather/pallas_call | solution.py:62
  143.9 7.8 %all-to-all-start = ((bf16[8,128,768]{2,1,0:T(8,128)(2,1)}), bf16[8,128,768]{2,1,0:T(8,128)(2,1)}, u32[]{:S(2)}, u32[]{:S(2)}) async-start(bf16[8,128,768]{2,1,0:T(8,128)(2,1)} %attend.3), calls=%async_computation | async-start | bytes 3145728 | tf_op jit(solution)/shard_map/all_to_all | solution.py:433
  151.7 11.2 %attend.4 = (bf16[128,768]{1,0:T(8,128)(2,1)}, bf16[128,768]{1,0:T(8,128)(2,1)}, bf16[128,768]{1,0:T(8,128)(2,1)}, bf16[128,768]{1,0:T(8,128)(2,1)}) custom-call(s32[8]{0:T(128)} %bitcast.24, s32[16,16]{1,0:T(8,128)} %bitcast.21, s32[3]{0:T(128)} %pad_add_fusion.position.refs_2_, bf16[3,128,768]{2,1,0:T(8,128)(2,1)} %get-tuple-element.94.refs_0_.refs_3_, ...), custom_call_target="tpu_custom_call" | custom-call | flops 1610612736 | bytes 9437184 | tf_op jit(solution)/shard_map/attend/pallas_call | solution.py:375
  162.9 6.9 %collective-permute-start.16 = (bf16[128,768]{1,0:T(8,128)(2,1)}, bf16[128,768]{1,0:T(8,128)(2,1)S(1)}, u32[]{:S(2)}, u32[]{:S(2)}) collective-permute-start(bf16[128,768]{1,0:T(8,128)(2,1)} %get-tuple-element.105), channel_id=1, source_target_pairs={{0,250},{1,251},{2,248},{3,249},{4,254},{5,255},{6,252},{7,253},{8... | collective-permute-start | bytes 589832 | tf_op jit(solution)/shard_map/ppermute | solution.py:414
  169.8 2.8 %collective-permute-start.17 = (bf16[128,768]{1,0:T(8,128)(2,1)}, bf16[128,768]{1,0:T(8,128)(2,1)S(1)}, u32[]{:S(2)}, u32[]{:S(2)}) collective-permute-start(bf16[128,768]{1,0:T(8,128)(2,1)} %get-tuple-element.106), channel_id=1, source_target_pairs={{0,252},{1,253},{2,254},{3,255},{4,248},{5,249},{6,250},{7,251},{8... | collective-permute-start | bytes 589832 | tf_op jit(solution)/shard_map/ppermute | solution.py:414
  172.6 6.1 %collective-permute-start.18 = (bf16[128,768]{1,0:T(8,128)(2,1)}, bf16[128,768]{1,0:T(8,128)(2,1)S(1)}, u32[]{:S(2)}, u32[]{:S(2)}) collective-permute-start(bf16[128,768]{1,0:T(8,128)(2,1)} %get-tuple-element.107), channel_id=1, source_target_pairs={{0,254},{1,255},{2,252},{3,253},{4,250},{5,251},{6,248},{7,249},{8... | collective-permute-start | bytes 589832 | tf_op jit(solution)/shard_map/ppermute | solution.py:414
  178.6 2.3 collective-permute-start.15
  180.9 9.9 %attend.5 = (bf16[128,768]{1,0:T(8,128)(2,1)}, bf16[128,768]{1,0:T(8,128)(2,1)}, bf16[128,768]{1,0:T(8,128)(2,1)}, bf16[128,768]{1,0:T(8,128)(2,1)}) custom-call(s32[8]{0:T(128)} %bitcast.25, s32[16,16]{1,0:T(8,128)} %bitcast.22, s32[3]{0:T(128)} %pad_add_fusion.position.refs_2_, bf16[3,128,768]{2,1,0:T(8,128)(2,1)} %get-tuple-element.94.refs_0_.refs_3_, ...), custom_call_target="tpu_custom_call" | custom-call | flops 1610612736 | bytes 9437184 | tf_op jit(solution)/shard_map/attend/pallas_call | solution.py:375
  192.6 3.8 %collective-permute-start.20 = (bf16[128,768]{1,0:T(8,128)(2,1)}, bf16[128,768]{1,0:T(8,128)(2,1)S(1)}, u32[]{:S(2)}, u32[]{:S(2)}) collective-permute-start(bf16[128,768]{1,0:T(8,128)(2,1)} %get-tuple-element.110), channel_id=1, source_target_pairs={{0,240},{1,241},{2,242},{3,243},{4,244},{5,245},{6,246},{7,247},{8... | collective-permute-start | bytes 589832 | tf_op jit(solution)/shard_map/ppermute | solution.py:414
  196.4 2.9 %collective-permute-start.21 = (bf16[128,768]{1,0:T(8,128)(2,1)}, bf16[128,768]{1,0:T(8,128)(2,1)S(1)}, u32[]{:S(2)}, u32[]{:S(2)}) collective-permute-start(bf16[128,768]{1,0:T(8,128)(2,1)} %get-tuple-element.111), channel_id=1, source_target_pairs={{0,242},{1,243},{2,240},{3,241},{4,246},{5,247},{6,244},{7,245},{8... | collective-permute-start | bytes 589832 | tf_op jit(solution)/shard_map/ppermute | solution.py:414
  199.3 2.3 collective-permute-start.22
  202.5 3.6 %collective-permute-done.21.refs_1_ = bf16[128,768]{1,0:T(8,128)(2,1)S(1)} collective-permute-done((bf16[128,768]{1,0:T(8,128)(2,1)}, bf16[128,768]{1,0:T(8,128)(2,1)S(1)}, u32[]{:S(2)}, u32[]{:S(2)}) %collective-permute-start.21) | collective-permute-done | bytes 196640 | tf_op jit(solution)/shard_map/ppermute | solution.py:414
  206.2 5.8 %collective-permute-done.22.refs_2_ = bf16[128,768]{1,0:T(8,128)(2,1)S(1)} collective-permute-done((bf16[128,768]{1,0:T(8,128)(2,1)}, bf16[128,768]{1,0:T(8,128)(2,1)S(1)}, u32[]{:S(2)}, u32[]{:S(2)}) %collective-permute-start.22) | collective-permute-done | bytes 196640 | tf_op jit(solution)/shard_map/ppermute | solution.py:414
  214.6 3.0 %join.3 = bf16[128,6144]{1,0:T(8,128)(2,1)} custom-call(s32[3]{0:T(128)} %pad_add_fusion.position.refs_2_, bf16[128,768]{1,0:T(8,128)(2,1)} %copy-done.12, bf16[128,768]{1,0:T(8,128)(2,1)} %copy-done.13, bf16[128,768]{1,0:T(8,128)(2,1)} %copy-done.14, bf16[128,768]{1,0:T(8,128)(2,1)} %copy-done.15, bf16[128,768]{1,0:T(8,128)(2,1)} %copy-done.11, ...), custom_call_target="tpu_custom_call" | custom-call | tf_op jit(solution)/shard_map/join/pallas_call | solution.py:62
  217.6 12.7 %collective-permute-done.19.refs_0_ = bf16[8,128,768]{2,1,0:T(8,128)(2,1)S(1)} collective-permute-done((bf16[8,128,768]{2,1,0:T(8,128)(2,1)}, bf16[8,128,768]{2,1,0:T(8,128)(2,1)S(1)}, u32[]{:S(2)}, u32[]{:S(2)}) %collective-permute-start.19) | collective-permute-done | bytes 1572896 | tf_op jit(solution)/shard_map/ppermute | solution.py:414
  231.5 3.0 %join.2 = bf16[128,6144]{1,0:T(8,128)(2,1)} custom-call(s32[3]{0:T(128)} %pad_add_fusion.position.refs_2_, bf16[8,128,768]{2,1,0:T(8,128)(2,1)} %copy-done.7), custom_call_target="tpu_custom_call" | custom-call | tf_op jit(solution)/shard_map/join/pallas_call | solution.py:62
  (63 shorter events, 20.5 us)
Async XLA Ops:
  4.6 54.8 %collective-permute-start.3 = (bf16[4,3,128,768]{3,2,1,0:T(8,128)(2,1)}, bf16[4,3,128,768]{3,2,1,0:T(8,128)(2,1)S(1)}, u32[]{:S(2)}, u32[]{:S(2)}) collective-permute-start(bf16[4,3,128,768]{3,2,1,0:T(8,128)(2,1)} %cut_side.1), channel_id=1, source_target_pairs={{0,8},{1,9},{2,10},{3,11},{4,12},{5,13},{6,14},{7,15},{8,0},{9,1},... | collective-permute-start | bytes 7077896 | tf_op jit(solution)/shard_map/ppermute | solution.py:414
  12.7 51.1 %collective-permute-start = (bf16[2,3,128,768]{3,2,1,0:T(8,128)(2,1)}, bf16[2,3,128,768]{3,2,1,0:T(8,128)(2,1)S(1)}, u32[]{:S(2)}, u32[]{:S(2)}) collective-permute-start(bf16[2,3,128,768]{3,2,1,0:T(8,128)(2,1)} %get-tuple-element.62), channel_id=1, source_target_pairs={{0,2},{1,3},{2,0},{3,1},{4,6},{5,7},{6,4},{7,5},{8,10},{9,11},{10,... | collective-permute-start | bytes 3538952 | tf_op jit(solution)/shard_map/ppermute | solution.py:414
  13.4 53.5 %collective-permute-start.1 = (bf16[2,3,128,768]{3,2,1,0:T(8,128)(2,1)}, bf16[2,3,128,768]{3,2,1,0:T(8,128)(2,1)}, u32[]{:S(2)}, u32[]{:S(2)}) collective-permute-start(bf16[2,3,128,768]{3,2,1,0:T(8,128)(2,1)} %get-tuple-element.63), channel_id=1, source_target_pairs={{0,4},{1,5},{2,6},{3,7},{4,0},{5,1},{6,2},{7,3},{8,12},{9,13},{10,... | collective-permute-start | bytes 3538952 | tf_op jit(solution)/shard_map/ppermute | solution.py:414
  15.8 52.5 %collective-permute-start.2 = (bf16[2,3,128,768]{3,2,1,0:T(8,128)(2,1)}, bf16[2,3,128,768]{3,2,1,0:T(8,128)(2,1)}, u32[]{:S(2)}, u32[]{:S(2)}) collective-permute-start(bf16[2,3,128,768]{3,2,1,0:T(8,128)(2,1)} %get-tuple-element.64), channel_id=1, source_target_pairs={{0,6},{1,7},{2,4},{3,5},{4,2},{5,3},{6,0},{7,1},{8,14},{9,15},{10,... | collective-permute-start | bytes 3538952 | tf_op jit(solution)/shard_map/ppermute | solution.py:414
  73.0 31.5 %collective-permute-start.7 = (bf16[4,3,128,768]{3,2,1,0:T(8,128)(2,1)}, bf16[4,3,128,768]{3,2,1,0:T(8,128)(2,1)}, u32[]{:S(2)}, u32[]{:S(2)}) collective-permute-start(bf16[4,3,128,768]{3,2,1,0:T(8,128)(2,1)} %get-tuple-element.84), channel_id=1, source_target_pairs={{0,1},{1,0},{2,3},{3,2},{4,5},{5,4},{6,7},{7,6},{8,9},{9,8},{10,11... | collective-permute-start | bytes 7077896 | tf_op jit(solution)/shard_map/ppermute | solution.py:414
  73.1 17.5 %collective-permute-start.4 = (bf16[3,128,768]{2,1,0:T(8,128)(2,1)}, bf16[3,128,768]{2,1,0:T(8,128)(2,1)S(1)}, u32[]{:S(2)}, u32[]{:S(2)}) collective-permute-start(bf16[3,128,768]{2,1,0:T(8,128)(2,1)} %get-tuple-element.73), channel_id=1, source_target_pairs={{0,2},{1,3},{2,0},{3,1},{4,6},{5,7},{6,4},{7,5},{8,10},{9,11},{10,... | collective-permute-start | bytes 1769480 | tf_op jit(solution)/shard_map/ppermute | solution.py:414
  76.2 26.2 %collective-permute-start.5 = (bf16[3,128,768]{2,1,0:T(8,128)(2,1)}, bf16[3,128,768]{2,1,0:T(8,128)(2,1)S(1)}, u32[]{:S(2)}, u32[]{:S(2)}) collective-permute-start(bf16[3,128,768]{2,1,0:T(8,128)(2,1)} %get-tuple-element.74), channel_id=1, source_target_pairs={{0,4},{1,5},{2,6},{3,7},{4,0},{5,1},{6,2},{7,3},{8,12},{9,13},{10,... | collective-permute-start | bytes 1769480 | tf_op jit(solution)/shard_map/ppermute | solution.py:414
  76.2 28.3 %collective-permute-start.6 = (bf16[3,128,768]{2,1,0:T(8,128)(2,1)}, bf16[3,128,768]{2,1,0:T(8,128)(2,1)}, u32[]{:S(2)}, u32[]{:S(2)}) collective-permute-start(bf16[3,128,768]{2,1,0:T(8,128)(2,1)} %get-tuple-element.75), channel_id=1, source_target_pairs={{0,6},{1,7},{2,4},{3,5},{4,2},{5,3},{6,0},{7,1},{8,14},{9,15},{10,... | collective-permute-start | bytes 1769480 | tf_op jit(solution)/shard_map/ppermute | solution.py:414
  77.8 54.6 %collective-permute-start.11 = (bf16[4,3,128,768]{3,2,1,0:T(8,128)(2,1)}, bf16[4,3,128,768]{3,2,1,0:T(8,128)(2,1)S(1)}, u32[]{:S(2)}, u32[]{:S(2)}) collective-permute-start(bf16[4,3,128,768]{3,2,1,0:T(8,128)(2,1)} %get-tuple-element.89), channel_id=1, source_target_pairs={{0,8},{1,9},{2,10},{3,11},{4,12},{5,13},{6,14},{7,15},{8,0},{9,1},... | collective-permute-start | bytes 7077896 | tf_op jit(solution)/shard_map/ppermute | solution.py:414
  90.6 14.0 %copy-start.5 = (bf16[3,128,768]{2,1,0:T(8,128)(2,1)}, bf16[3,128,768]{2,1,0:T(8,128)(2,1)S(1)}, u32[]{:S(2)}) copy-start(bf16[3,128,768]{2,1,0:T(8,128)(2,1)S(1)} %collective-permute-done.4.refs_1_.refs_8_) | copy-start | bytes 1769476
  107.5 5.2 %collective-permute-start.12 = (bf16[4,2,128,768]{3,2,1,0:T(8,128)(2,1)}, bf16[4,2,128,768]{3,2,1,0:T(8,128)(2,1)}, u32[]{:S(2)}, u32[]{:S(2)}) collective-permute-start(bf16[4,2,128,768]{3,2,1,0:T(8,128)(2,1)} %gather.2), channel_id=1, source_target_pairs={{0,1},{1,0},{2,3},{3,2},{4,5},{5,4},{6,7},{7,6},{8,9},{9,8},{10,11... | collective-permute-start | bytes 4718600 | tf_op jit(solution)/shard_map/ppermute | solution.py:414
  107.6 24.9 %collective-permute-start.8 = (bf16[3,128,768]{2,1,0:T(8,128)(2,1)}, bf16[3,128,768]{2,1,0:T(8,128)(2,1)S(1)}, u32[]{:S(2)}, u32[]{:S(2)}) collective-permute-start(bf16[3,128,768]{2,1,0:T(8,128)(2,1)} %get-tuple-element.86), channel_id=1, source_target_pairs={{0,2},{1,3},{2,0},{3,1},{4,6},{5,7},{6,4},{7,5},{8,10},{9,11},{10,... | collective-permute-start | bytes 1769480 | tf_op jit(solution)/shard_map/ppermute | solution.py:414
  110.5 28.4 %collective-permute-start.9 = (bf16[3,128,768]{2,1,0:T(8,128)(2,1)}, bf16[3,128,768]{2,1,0:T(8,128)(2,1)S(1)}, u32[]{:S(2)}, u32[]{:S(2)}) collective-permute-start(bf16[3,128,768]{2,1,0:T(8,128)(2,1)} %get-tuple-element.87), channel_id=1, source_target_pairs={{0,4},{1,5},{2,6},{3,7},{4,0},{5,1},{6,2},{7,3},{8,12},{9,13},{10,... | collective-permute-start | bytes 1769480 | tf_op jit(solution)/shard_map/ppermute | solution.py:414
  112.2 28.2 %collective-permute-start.10 = (bf16[3,128,768]{2,1,0:T(8,128)(2,1)}, bf16[3,128,768]{2,1,0:T(8,128)(2,1)}, u32[]{:S(2)}, u32[]{:S(2)}) collective-permute-start(bf16[3,128,768]{2,1,0:T(8,128)(2,1)} %get-tuple-element.88), channel_id=1, source_target_pairs={{0,6},{1,7},{2,4},{3,5},{4,2},{5,3},{6,0},{7,1},{8,14},{9,15},{10,... | collective-permute-start | bytes 1769480 | tf_op jit(solution)/shard_map/ppermute | solution.py:414
  132.4 10.9 %copy-start = (bf16[4,3,128,768]{3,2,1,0:T(8,128)(2,1)}, bf16[4,3,128,768]{3,2,1,0:T(8,128)(2,1)S(1)}, u32[]{:S(2)}) copy-start(bf16[4,3,128,768]{3,2,1,0:T(8,128)(2,1)S(1)} %collective-permute-done.11.refs_7_.refs_8_.refs_9_.refs_10_) | copy-start | bytes 7077892
  140.4 11.2 %collective-permute-start.14 = (bf16[4,3,128,768]{3,2,1,0:T(8,128)(2,1)S(1)}, bf16[4,3,128,768]{3,2,1,0:T(8,128)(2,1)}, u32[]{:S(2)}, u32[]{:S(2)}) collective-permute-start(bf16[4,3,128,768]{3,2,1,0:T(8,128)(2,1)S(1)} %collective-permute-done.11.refs_7_.refs_8_.refs_9_.refs_10_), channel_id=1, source_target_pairs={{0,1},{1,0},{2,3},{3,2},{4,5},{5,4},{6,7},{7,6},{8,9},{9,8},{10,11... | collective-permute-start | bytes 7077896 | tf_op jit(solution)/shard_map/ppermute | solution.py:414
  143.3 8.4 %collective-permute-start.13 = (bf16[4,2,128,768]{3,2,1,0:T(8,128)(2,1)}, bf16[4,2,128,768]{3,2,1,0:T(8,128)(2,1)}, u32[]{:S(2)}, u32[]{:S(2)}) collective-permute-start(bf16[4,2,128,768]{3,2,1,0:T(8,128)(2,1)} %gather.3), channel_id=1, source_target_pairs={{0,1},{1,0},{2,3},{3,2},{4,5},{5,4},{6,7},{7,6},{8,9},{9,8},{10,11... | collective-permute-start | bytes 4718600 | tf_op jit(solution)/shard_map/ppermute | solution.py:414
  143.9 46.9 %all-to-all-start = ((bf16[8,128,768]{2,1,0:T(8,128)(2,1)}), bf16[8,128,768]{2,1,0:T(8,128)(2,1)}, u32[]{:S(2)}, u32[]{:S(2)}) async-start(bf16[8,128,768]{2,1,0:T(8,128)(2,1)} %attend.3), calls=%async_computation | async-start | bytes 3145728 | tf_op jit(solution)/shard_map/all_to_all | solution.py:433
  162.9 27.9 %collective-permute-start.16 = (bf16[128,768]{1,0:T(8,128)(2,1)}, bf16[128,768]{1,0:T(8,128)(2,1)S(1)}, u32[]{:S(2)}, u32[]{:S(2)}) collective-permute-start(bf16[128,768]{1,0:T(8,128)(2,1)} %get-tuple-element.105), channel_id=1, source_target_pairs={{0,250},{1,251},{2,248},{3,249},{4,254},{5,255},{6,252},{7,253},{8... | collective-permute-start | bytes 589832 | tf_op jit(solution)/shard_map/ppermute | solution.py:414
  169.8 21.1 %collective-permute-start.17 = (bf16[128,768]{1,0:T(8,128)(2,1)}, bf16[128,768]{1,0:T(8,128)(2,1)S(1)}, u32[]{:S(2)}, u32[]{:S(2)}) collective-permute-start(bf16[128,768]{1,0:T(8,128)(2,1)} %get-tuple-element.106), channel_id=1, source_target_pairs={{0,252},{1,253},{2,254},{3,255},{4,248},{5,249},{6,250},{7,251},{8... | collective-permute-start | bytes 589832 | tf_op jit(solution)/shard_map/ppermute | solution.py:414
  172.6 18.3 %collective-permute-start.18 = (bf16[128,768]{1,0:T(8,128)(2,1)}, bf16[128,768]{1,0:T(8,128)(2,1)S(1)}, u32[]{:S(2)}, u32[]{:S(2)}) collective-permute-start(bf16[128,768]{1,0:T(8,128)(2,1)} %get-tuple-element.107), channel_id=1, source_target_pairs={{0,254},{1,255},{2,252},{3,253},{4,250},{5,251},{6,248},{7,249},{8... | collective-permute-start | bytes 589832 | tf_op jit(solution)/shard_map/ppermute | solution.py:414
  178.6 12.2 %collective-permute-start.15 = (bf16[128,768]{1,0:T(8,128)(2,1)}, bf16[128,768]{1,0:T(8,128)(2,1)S(1)}, u32[]{:S(2)}, u32[]{:S(2)}) collective-permute-start(bf16[128,768]{1,0:T(8,128)(2,1)} %get-tuple-element.99), channel_id=1, source_target_pairs={{0,248},{1,249},{2,250},{3,251},{4,252},{5,253},{6,254},{7,255},{8... | collective-permute-start | bytes 589832 | tf_op jit(solution)/shard_map/ppermute | solution.py:414
  190.8 23.1 %copy-start.8 = (bf16[128,768]{1,0:T(8,128)(2,1)}, bf16[128,768]{1,0:T(8,128)(2,1)S(1)}, u32[]{:S(2)}) copy-start(bf16[128,768]{1,0:T(8,128)(2,1)S(1)} %collective-permute-done.16.refs_5_) | copy-start | bytes 589828
  190.9 23.1 %copy-start.9 = (bf16[128,768]{1,0:T(8,128)(2,1)}, bf16[128,768]{1,0:T(8,128)(2,1)S(1)}, u32[]{:S(2)}) copy-start(bf16[128,768]{1,0:T(8,128)(2,1)S(1)} %collective-permute-done.17.refs_6_) | copy-start | bytes 589828
  190.9 23.0 %copy-start.10 = (bf16[128,768]{1,0:T(8,128)(2,1)}, bf16[128,768]{1,0:T(8,128)(2,1)S(1)}, u32[]{:S(2)}) copy-start(bf16[128,768]{1,0:T(8,128)(2,1)S(1)} %collective-permute-done.18.refs_7_) | copy-start | bytes 589828
  190.9 23.0 %copy-start.11 = (bf16[128,768]{1,0:T(8,128)(2,1)}, bf16[128,768]{1,0:T(8,128)(2,1)S(1)}, u32[]{:S(2)}) copy-start(bf16[128,768]{1,0:T(8,128)(2,1)S(1)} %collective-permute-done.15.refs_4_) | copy-start | bytes 589828
  190.9 39.4 %collective-permute-start.19 = (bf16[8,128,768]{2,1,0:T(8,128)(2,1)}, bf16[8,128,768]{2,1,0:T(8,128)(2,1)S(1)}, u32[]{:S(2)}, u32[]{:S(2)}) collective-permute-start(bf16[8,128,768]{2,1,0:T(8,128)(2,1)} %all-to-all-done), channel_id=1, source_target_pairs={{0,16},{1,17},{2,18},{3,19},{4,20},{5,21},{6,22},{7,23},{8,24},{9,... | collective-permute-start | bytes 4718600 | tf_op jit(solution)/shard_map/ppermute | solution.py:414
  192.6 9.9 %collective-permute-start.20 = (bf16[128,768]{1,0:T(8,128)(2,1)}, bf16[128,768]{1,0:T(8,128)(2,1)S(1)}, u32[]{:S(2)}, u32[]{:S(2)}) collective-permute-start(bf16[128,768]{1,0:T(8,128)(2,1)} %get-tuple-element.110), channel_id=1, source_target_pairs={{0,240},{1,241},{2,242},{3,243},{4,244},{5,245},{6,246},{7,247},{8... | collective-permute-start | bytes 589832 | tf_op jit(solution)/shard_map/ppermute | solution.py:414
  196.4 9.8 %collective-permute-start.21 = (bf16[128,768]{1,0:T(8,128)(2,1)}, bf16[128,768]{1,0:T(8,128)(2,1)S(1)}, u32[]{:S(2)}, u32[]{:S(2)}) collective-permute-start(bf16[128,768]{1,0:T(8,128)(2,1)} %get-tuple-element.111), channel_id=1, source_target_pairs={{0,242},{1,243},{2,240},{3,241},{4,246},{5,247},{6,244},{7,245},{8... | collective-permute-start | bytes 589832 | tf_op jit(solution)/shard_map/ppermute | solution.py:414
  199.3 12.7 %collective-permute-start.22 = (bf16[128,768]{1,0:T(8,128)(2,1)}, bf16[128,768]{1,0:T(8,128)(2,1)S(1)}, u32[]{:S(2)}, u32[]{:S(2)}) collective-permute-start(bf16[128,768]{1,0:T(8,128)(2,1)} %get-tuple-element.112), channel_id=1, source_target_pairs={{0,244},{1,245},{2,246},{3,247},{4,240},{5,241},{6,242},{7,243},{8... | collective-permute-start | bytes 589832 | tf_op jit(solution)/shard_map/ppermute | solution.py:414
  201.6 12.3 %collective-permute-start.23 = (bf16[128,768]{1,0:T(8,128)(2,1)}, bf16[128,768]{1,0:T(8,128)(2,1)S(1)}, u32[]{:S(2)}, u32[]{:S(2)}) collective-permute-start(bf16[128,768]{1,0:T(8,128)(2,1)} %get-tuple-element.113), channel_id=1, source_target_pairs={{0,246},{1,247},{2,244},{3,245},{4,242},{5,243},{6,240},{7,241},{8... | collective-permute-start | bytes 589832 | tf_op jit(solution)/shard_map/ppermute | solution.py:414
  202.5 11.4 %copy-start.12 = (bf16[128,768]{1,0:T(8,128)(2,1)}, bf16[128,768]{1,0:T(8,128)(2,1)S(1)}, u32[]{:S(2)}) copy-start(bf16[128,768]{1,0:T(8,128)(2,1)S(1)} %collective-permute-done.20.refs_0_) | copy-start | bytes 589828
  (9 other events, 29.1 us)
